TPU v7x, 32 devices: a whole 2x2x4 slice. The times are simulated.
32 devices in a mesh: dp: 4 (over y, core), fsdp: 8 (over z, x).
Axes of the slice: x: 2, y: 2, z: 4, core: 2. Of those that a mesh axis runs over, the one named last changes fastest.
Arguments:
- images: bfloat16 [32, 26, 38, 768], P(('dp', 'fsdp')), may hold values from -6 to 6
- grad_out: bfloat16 [32, 26, 38, 768], P(('dp', 'fsdp')), may hold values from -6 to 6
- box_rows: int32 [32, 300, 2], P(('dp', 'fsdp')), may hold values from 0 to 26
- box_cols: int32 [32, 300, 2], P(('dp', 'fsdp')), may hold values from 0 to 38
- box_valid: int32 [32, 300], P(('dp', 'fsdp')), may hold values 0 or 1
- box_count: int32 [32], P(('dp', 'fsdp')), may hold values from 1 to 300
- in_weight: bfloat16 [768, 2304], P(('dp', 'fsdp')), may hold values from -0.21875 to 0.21875
- query_bias: bfloat16 [768], P(('dp', 'fsdp')), may hold values from -2 to 2
- value_bias: bfloat16 [768], P(('dp', 'fsdp')), may hold values from -2 to 2
- out_weight: bfloat16 [768, 768], P(('dp', 'fsdp')), may hold values from -1.75 to 1.75
- out_bias: bfloat16 [768], P(('dp', 'fsdp')), may hold values from -2 to 2
- first_gain: bfloat16 [768], P(('dp', 'fsdp')), may hold values from 0.099609375 to 1.8984375
- first_shift: bfloat16 [768], P(('dp', 'fsdp')), may hold values from -2 to 2
- second_gain: bfloat16 [768], P(('dp', 'fsdp')), may hold values from 0.099609375 to 1.8984375
- second_shift: bfloat16 [768], P(('dp', 'fsdp')), may hold values from -2 to 2
- up_weight: bfloat16 [768, 3072], P(('dp', 'fsdp')), may hold values from -0.21875 to 0.21875
- up_bias: bfloat16 [3072], P(('dp', 'fsdp')), may hold values from -2 to 2
- down_weight: bfloat16 [3072, 768], P(('dp', 'fsdp')), may hold values from -0.109375 to 0.109375
- down_bias: bfloat16 [768], P(('dp', 'fsdp')), may hold values from -2 to 2
- row_table: bfloat16 [27, 64], replicated, may hold values from -1 to 1
- col_table: bfloat16 [27, 64], replicated, may hold values from -1 to 1
Outputs:
- block_out: bfloat16 [32, 26, 38, 768], P(('dp', 'fsdp'))
- image_grad: bfloat16 [32, 26, 38, 768], P(('dp', 'fsdp'))
- in_weight_grad: float32 [768, 2304], P(('dp', 'fsdp'))
- query_bias_grad: float32 [768], P(('dp', 'fsdp'))
- value_bias_grad: float32 [768], P(('dp', 'fsdp'))
- out_weight_grad: float32 [768, 768], P(('dp', 'fsdp'))
- out_bias_grad: float32 [768], P(('dp', 'fsdp'))
- first_gain_grad: float32 [768], P(('dp', 'fsdp'))
- first_shift_grad: float32 [768], P(('dp', 'fsdp'))
- second_gain_grad: float32 [768], P(('dp', 'fsdp'))
- second_shift_grad: float32 [768], P(('dp', 'fsdp'))
- up_weight_grad: float32 [768, 3072], P(('dp', 'fsdp'))
- up_bias_grad: float32 [3072], P(('dp', 'fsdp'))
- down_weight_grad: float32 [3072, 768], P(('dp', 'fsdp'))
- down_bias_grad: float32 [768], P(('dp', 'fsdp'))
- row_table_grad: float32 [27, 64], replicated
- col_table_grad: float32 [27, 64], replicated
All inputs are finite; a program needn't handle non-finite values. No bound on the sum of `box_valid` on one device may be relied on, other than what follows from the above.
Results may differ from a plain program's by a relative error of at most 0.013.
Values may be sent and summed in bfloat16 or wider, within the bound.
No kernel may reach another device: no remote copies, remote signals or barrier semaphores. Data moves between devices by JAX's collectives and lax.ppermute only.
A program may use at most 256 MiB of HBM per device.

v0:
```python
import jax
import jax.numpy as jnp
from jax import lax
from jax.sharding import PartitionSpec as P

D = 768
HEADS = 12
HD = 64
WIN = 14
GH = 26
GW = 38
NBOX = 300
HP = 28
WP = 42


epsilon = 1e-06
highest = lax.Precision.HIGHEST


def normalize(tensor):
    center = tensor - jnp.mean(tensor, axis=-1, keepdims=True)
    inverse = lax.rsqrt(jnp.mean(center * center, axis=-1, keepdims=True) + epsilon)
    return (center * inverse, inverse)


def norm_back(grad_normed, unit_norm, inverse, gain_vec):
    scaled = grad_normed * gain_vec
    return inverse * (
        scaled
        - jnp.mean(scaled, axis=-1, keepdims=True)
        - unit_norm * jnp.mean(scaled * unit_norm, axis=-1, keepdims=True)
    )


def windows_of(field_in):
    number = field_in.shape[0]
    width = field_in.shape[-1]
    padded = jnp.pad(field_in, ((0, 0), (0, HP - GH), (0, WP - GW), (0, 0)))
    pieces = padded.reshape(number, HP // WIN, WIN, WP // WIN, WIN, width)
    return pieces.transpose(0, 1, 3, 2, 4, 5).reshape(-1, WIN * WIN, width)


def field_of(pieces, number):
    width = pieces.shape[-1]
    layout = pieces.reshape(number, HP // WIN, WP // WIN, WIN, WIN, width).transpose(
        0, 1, 3, 2, 4, 5
    )
    return layout.reshape(number, HP, WP, width)[:, :GH, :GW, :]


def pair_pickers():
    places = jnp.arange(WIN * WIN, dtype=jnp.int32)
    row_of = places // WIN
    col_of = places % WIN
    entries = jnp.arange(2 * WIN - 1, dtype=jnp.int32)
    row_offsets = row_of[:, None] - row_of[None, :] + WIN - 1
    col_offsets = col_of[:, None] - col_of[None, :] + WIN - 1
    row_pick = (row_offsets[:, :, None] == entries[None, None, :]).astype(jnp.float32)
    col_pick = (col_offsets[:, :, None] == entries[None, None, :]).astype(jnp.float32)
    return (row_pick, col_pick)


def patch_weights(rows, cols, valid, number):
    slot_ids = jnp.arange(NBOX, dtype=jnp.int32)
    live_box = ((slot_ids < number) & (valid == 1)).astype(jnp.float32)
    top_row = jnp.minimum(rows[:, 0], rows[:, 1])
    low_row = jnp.maximum(rows[:, 0], rows[:, 1])
    left_col = jnp.minimum(cols[:, 0], cols[:, 1])
    right_col = jnp.maximum(cols[:, 0], cols[:, 1])
    grid_rows = jnp.arange(GH, dtype=jnp.int32)
    grid_cols = jnp.arange(GW, dtype=jnp.int32)
    in_rows = (
        (grid_rows[None, :] >= top_row[:, None]) & (grid_rows[None, :] < low_row[:, None])
    ).astype(jnp.float32) * live_box[:, None]
    in_cols = (
        (grid_cols[None, :] >= left_col[:, None]) & (grid_cols[None, :] < right_col[:, None])
    ).astype(jnp.float32)
    inside = jnp.dot(in_rows.T, in_cols, precision=highest)
    return 1.0 + 2.0 * inside / jnp.maximum(jnp.sum(live_box), 1.0)


def score_block(window_block, in_weight, bias_all, rows_low, cols_low):
    number = window_block.shape[0]
    span = WIN * WIN
    packed = (
        jnp.dot(window_block.reshape(-1, D), in_weight, preferred_element_type=jnp.float32)
        + bias_all
    )
    packed = packed.astype(jnp.bfloat16).reshape(number, span, 3, HEADS, HD)
    queries = packed[:, :, 0]
    key_rows = packed[:, :, 1]
    values = packed[:, :, 2]
    scores = jnp.einsum(
        "wqhc,wkhc->whqk", queries, key_rows, preferred_element_type=jnp.float32
    ) * HD ** (-0.5)
    scores = scores + jnp.einsum(
        "wqhc,qkc->whqk", queries, rows_low, preferred_element_type=jnp.float32
    )
    scores = scores + jnp.einsum(
        "wqhc,qkc->whqk", queries, cols_low, preferred_element_type=jnp.float32
    )
    return (queries, key_rows, values, scores)


def local(
    images,
    grad_out,
    box_rows,
    box_cols,
    box_valid,
    box_count,
    in_weight,
    query_bias,
    value_bias,
    out_weight,
    out_bias,
    first_gain,
    first_shift,
    second_gain,
    second_shift,
    up_weight,
    up_bias,
    down_weight,
    down_bias,
    row_table,
    col_table,
):
    gathered = (
        lax.all_gather(in_weight, ("dp", "fsdp"), axis=0, tiled=True),
        lax.all_gather(query_bias, ("dp", "fsdp"), axis=0, tiled=True),
        lax.all_gather(value_bias, ("dp", "fsdp"), axis=0, tiled=True),
        lax.all_gather(out_weight, ("dp", "fsdp"), axis=0, tiled=True),
        lax.all_gather(out_bias, ("dp", "fsdp"), axis=0, tiled=True),
        lax.all_gather(first_gain, ("dp", "fsdp"), axis=0, tiled=True),
        lax.all_gather(first_shift, ("dp", "fsdp"), axis=0, tiled=True),
        lax.all_gather(second_gain, ("dp", "fsdp"), axis=0, tiled=True),
        lax.all_gather(second_shift, ("dp", "fsdp"), axis=0, tiled=True),
        lax.all_gather(up_weight, ("dp", "fsdp"), axis=0, tiled=True),
        lax.all_gather(up_bias, ("dp", "fsdp"), axis=0, tiled=True),
        lax.all_gather(down_weight, ("dp", "fsdp"), axis=0, tiled=True),
        lax.all_gather(down_bias, ("dp", "fsdp"), axis=0, tiled=True),
    )
    images_here = images.shape[0]
    per_row = WP // WIN
    span = WIN * WIN
    row_pick, col_pick = pair_pickers()
    rows_low = jnp.einsum(
        "qkr,rc->qkc", row_pick, row_table.astype(jnp.float32), precision=highest
    ).astype(jnp.bfloat16)
    cols_low = jnp.einsum(
        "qkr,rc->qkc", col_pick, col_table.astype(jnp.float32), precision=highest
    ).astype(jnp.bfloat16)

    def biases_of(weights_all):
        query_part = weights_all[1].astype(jnp.float32)
        return jnp.concatenate(
            [query_part, jnp.zeros_like(query_part), weights_all[2].astype(jnp.float32)]
        )

    field_in = images.astype(jnp.float32)
    unit_one, inverse_one = normalize(field_in)
    gain_one = gathered[5].astype(jnp.float32)
    normed_one = unit_one * gain_one + gathered[6].astype(jnp.float32)
    windows = windows_of(normed_one).astype(jnp.bfloat16)
    blocks = windows.reshape(-1, per_row, span, D)
    bias_fwd = biases_of(gathered)

    def forward_block(window_block):
        number = window_block.shape[0]
        queries, key_rows, values, scores = score_block(
            window_block, gathered[0], bias_fwd, rows_low, cols_low
        )
        log_total = jax.nn.logsumexp(scores, axis=-1)
        soft = jnp.exp(scores - log_total[..., None]).astype(jnp.bfloat16)
        attended = jnp.einsum("whqk,wkhc->wqhc", soft, values, preferred_element_type=jnp.float32)
        return (attended.astype(jnp.bfloat16).reshape(number * span, D), log_total)

    attended_all, log_totals = lax.map(forward_block, blocks)
    branch = jnp.dot(
        attended_all.reshape(-1, D), gathered[3], preferred_element_type=jnp.float32
    ) + gathered[4].astype(jnp.float32)
    branch = field_of(branch.reshape(-1, span, D), images_here)
    middle = field_in + branch
    unit_two, inverse_two = normalize(middle)
    gain_two = gathered[7].astype(jnp.float32)
    normed_two = (
        (unit_two * gain_two + gathered[8].astype(jnp.float32)).astype(jnp.bfloat16).reshape(-1, D)
    )
    hidden = jnp.dot(normed_two, gathered[9], preferred_element_type=jnp.float32) + gathered[
        10
    ].astype(jnp.float32)
    active = jax.nn.gelu(hidden, approximate=False).astype(jnp.bfloat16)
    update = jnp.dot(active, gathered[11], preferred_element_type=jnp.float32) + gathered[
        12
    ].astype(jnp.float32)
    block_out = (middle + update.reshape(middle.shape)).astype(jnp.bfloat16)
    weights_back = (
        lax.all_gather(in_weight, ("dp", "fsdp"), axis=0, tiled=True),
        lax.all_gather(query_bias, ("dp", "fsdp"), axis=0, tiled=True),
        lax.all_gather(value_bias, ("dp", "fsdp"), axis=0, tiled=True),
        lax.all_gather(out_weight, ("dp", "fsdp"), axis=0, tiled=True),
        lax.all_gather(out_bias, ("dp", "fsdp"), axis=0, tiled=True),
        lax.all_gather(first_gain, ("dp", "fsdp"), axis=0, tiled=True),
        lax.all_gather(first_shift, ("dp", "fsdp"), axis=0, tiled=True),
        lax.all_gather(second_gain, ("dp", "fsdp"), axis=0, tiled=True),
        lax.all_gather(second_shift, ("dp", "fsdp"), axis=0, tiled=True),
        lax.all_gather(up_weight, ("dp", "fsdp"), axis=0, tiled=True),
        lax.all_gather(up_bias, ("dp", "fsdp"), axis=0, tiled=True),
        lax.all_gather(down_weight, ("dp", "fsdp"), axis=0, tiled=True),
        lax.all_gather(down_bias, ("dp", "fsdp"), axis=0, tiled=True),
    )
    weighting = jax.vmap(patch_weights)(box_rows, box_cols, box_valid, box_count)
    cotangent = grad_out.astype(jnp.float32) * weighting[..., None]
    grad_update = cotangent.astype(jnp.bfloat16).reshape(-1, D)
    down_bias_grad = jnp.sum(grad_update.astype(jnp.float32), axis=0)
    down_weight_grad = jnp.einsum(
        "rf,rd->fd", active, grad_update, preferred_element_type=jnp.float32
    )
    grad_active = jnp.einsum(
        "rd,fd->rf", grad_update, weights_back[11], preferred_element_type=jnp.float32
    )
    unused_value, gelu_back = jax.vjp(lambda tensor: jax.nn.gelu(tensor, approximate=False), hidden)
    grad_hidden = gelu_back(grad_active)[0].astype(jnp.bfloat16)
    up_bias_grad = jnp.sum(grad_hidden.astype(jnp.float32), axis=0)
    up_weight_grad = jnp.einsum(
        "rd,rf->df", normed_two, grad_hidden, preferred_element_type=jnp.float32
    )
    grad_norm_two = jnp.einsum(
        "rf,df->rd", grad_hidden, weights_back[9], preferred_element_type=jnp.float32
    ).reshape(middle.shape)
    flat_unit_two = unit_two.reshape(-1, D)
    second_gain_grad = jnp.sum(grad_norm_two.reshape(-1, D) * flat_unit_two, axis=0)
    second_shift_grad = jnp.sum(grad_norm_two.reshape(-1, D), axis=0)
    grad_middle = cotangent + norm_back(
        grad_norm_two, unit_two, inverse_two, weights_back[7].astype(jnp.float32)
    )
    grad_branch = grad_middle.astype(jnp.bfloat16)
    out_bias_grad = jnp.sum(grad_branch.astype(jnp.float32).reshape(-1, D), axis=0)
    branch_blocks = windows_of(grad_branch).reshape(-1, per_row * span, D)
    bias_back = biases_of(weights_back)

    def backward_block(carry, item):
        grad_in, grad_qbias, grad_vbias, grad_out_w, grad_pairs = carry
        window_block, log_total, grad_piece = item
        number = window_block.shape[0]
        queries, key_rows, values, scores = score_block(
            window_block, weights_back[0], bias_back, rows_low, cols_low
        )
        probs = jnp.exp(scores - log_total[..., None])
        soft = probs.astype(jnp.bfloat16)
        attended = jnp.einsum("whqk,wkhc->wqhc", soft, values, preferred_element_type=jnp.float32)
        attended = attended.astype(jnp.bfloat16).reshape(number * span, D)
        grad_out_w = grad_out_w + jnp.einsum(
            "rd,re->de", attended, grad_piece, preferred_element_type=jnp.float32
        )
        grad_attended = jnp.einsum(
            "re,de->rd", grad_piece, weights_back[3], preferred_element_type=jnp.float32
        )
        grad_attended = grad_attended.astype(jnp.bfloat16).reshape(number, span, HEADS, HD)
        grad_values = jnp.einsum(
            "whqk,wqhc->wkhc", soft, grad_attended, preferred_element_type=jnp.float32
        )
        grad_probs = jnp.einsum(
            "wqhc,wkhc->whqk", grad_attended, values, preferred_element_type=jnp.float32
        )
        grad_scores = probs * (grad_probs - jnp.sum(grad_probs * probs, axis=-1, keepdims=True))
        grad_scores = grad_scores.astype(jnp.bfloat16)
        grad_queries = jnp.einsum(
            "whqk,wkhc->wqhc", grad_scores, key_rows, preferred_element_type=jnp.float32
        ) * HD ** (-0.5)
        grad_keys = jnp.einsum(
            "whqk,wqhc->wkhc", grad_scores, queries, preferred_element_type=jnp.float32
        ) * HD ** (-0.5)
        grad_queries = grad_queries + jnp.einsum(
            "whqk,qkc->wqhc", grad_scores, rows_low, preferred_element_type=jnp.float32
        )
        grad_queries = grad_queries + jnp.einsum(
            "whqk,qkc->wqhc", grad_scores, cols_low, preferred_element_type=jnp.float32
        )
        grad_pairs = grad_pairs + jnp.einsum(
            "whqk,wqhc->qkc", grad_scores, queries, preferred_element_type=jnp.float32
        )
        grad_packed = jnp.stack([grad_queries, grad_keys, grad_values], axis=2).reshape(
            number * span, 3 * D
        )
        grad_packed = grad_packed.astype(jnp.bfloat16)
        packed_wide = grad_packed.astype(jnp.float32)
        grad_qbias = grad_qbias + jnp.sum(packed_wide[:, :D], axis=0)
        grad_vbias = grad_vbias + jnp.sum(packed_wide[:, 2 * D :], axis=0)
        grad_in = grad_in + jnp.einsum(
            "rd,re->de",
            window_block.reshape(-1, D),
            grad_packed,
            preferred_element_type=jnp.float32,
        )
        grad_windows = jnp.einsum(
            "re,de->rd", grad_packed, weights_back[0], preferred_element_type=jnp.float32
        )
        return ((grad_in, grad_qbias, grad_vbias, grad_out_w, grad_pairs), grad_windows)

    start = (
        jnp.zeros((D, 3 * D), jnp.float32),
        jnp.zeros((D,), jnp.float32),
        jnp.zeros((D,), jnp.float32),
        jnp.zeros((D, D), jnp.float32),
        jnp.zeros((span, span, HD), jnp.float32),
    )
    totals, grad_windows = lax.scan(backward_block, start, (blocks, log_totals, branch_blocks))
    in_weight_grad, query_bias_grad, value_bias_grad, out_weight_grad, pair_totals = totals
    grad_norm_one = field_of(grad_windows.reshape(-1, span, D), images_here)
    first_gain_grad = jnp.sum((grad_norm_one * unit_one).reshape(-1, D), axis=0)
    first_shift_grad = jnp.sum(grad_norm_one.reshape(-1, D), axis=0)
    image_grad = (
        grad_middle
        + norm_back(grad_norm_one, unit_one, inverse_one, weights_back[5].astype(jnp.float32))
    ).astype(jnp.bfloat16)
    row_terms = jnp.einsum("qkr,qkc->rc", row_pick, pair_totals, precision=highest)
    col_terms = jnp.einsum("qkr,qkc->rc", col_pick, pair_totals, precision=highest)
    row_table_grad, col_table_grad = lax.psum((row_terms, col_terms), ("dp", "fsdp"))
    owned = (
        lax.psum_scatter(in_weight_grad, ("dp", "fsdp"), scatter_dimension=0, tiled=True),
        lax.psum_scatter(query_bias_grad, ("dp", "fsdp"), scatter_dimension=0, tiled=True),
        lax.psum_scatter(value_bias_grad, ("dp", "fsdp"), scatter_dimension=0, tiled=True),
        lax.psum_scatter(out_weight_grad, ("dp", "fsdp"), scatter_dimension=0, tiled=True),
        lax.psum_scatter(out_bias_grad, ("dp", "fsdp"), scatter_dimension=0, tiled=True),
        lax.psum_scatter(first_gain_grad, ("dp", "fsdp"), scatter_dimension=0, tiled=True),
        lax.psum_scatter(first_shift_grad, ("dp", "fsdp"), scatter_dimension=0, tiled=True),
        lax.psum_scatter(second_gain_grad, ("dp", "fsdp"), scatter_dimension=0, tiled=True),
        lax.psum_scatter(second_shift_grad, ("dp", "fsdp"), scatter_dimension=0, tiled=True),
        lax.psum_scatter(up_weight_grad, ("dp", "fsdp"), scatter_dimension=0, tiled=True),
        lax.psum_scatter(up_bias_grad, ("dp", "fsdp"), scatter_dimension=0, tiled=True),
        lax.psum_scatter(down_weight_grad, ("dp", "fsdp"), scatter_dimension=0, tiled=True),
        lax.psum_scatter(down_bias_grad, ("dp", "fsdp"), scatter_dimension=0, tiled=True),
    )
    return (
        block_out,
        image_grad,
        owned[0],
        owned[1],
        owned[2],
        owned[3],
        owned[4],
        owned[5],
        owned[6],
        owned[7],
        owned[8],
        owned[9],
        owned[10],
        owned[11],
        owned[12],
        row_table_grad,
        col_table_grad,
    )


def solution(mesh):
    return jax.shard_map(
        local,
        mesh=mesh,
        in_specs=(
            P(("dp", "fsdp"), None, None, None),
            P(("dp", "fsdp"), None, None, None),
            P(("dp", "fsdp"), None, None),
            P(("dp", "fsdp"), None, None),
            P(("dp", "fsdp"), None),
            P(("dp", "fsdp")),
            P(("dp", "fsdp"), None),
            P(("dp", "fsdp")),
            P(("dp", "fsdp")),
            P(("dp", "fsdp"), None),
            P(("dp", "fsdp")),
            P(("dp", "fsdp")),
            P(("dp", "fsdp")),
            P(("dp", "fsdp")),
            P(("dp", "fsdp")),
            P(("dp", "fsdp"), None),
            P(("dp", "fsdp")),
            P(("dp", "fsdp"), None),
            P(("dp", "fsdp")),
            P(),
            P(),
        ),
        out_specs=(
            P(("dp", "fsdp"), None, None, None),
            P(("dp", "fsdp"), None, None, None),
            P(("dp", "fsdp"), None),
            P(("dp", "fsdp")),
            P(("dp", "fsdp")),
            P(("dp", "fsdp"), None),
            P(("dp", "fsdp")),
            P(("dp", "fsdp")),
            P(("dp", "fsdp")),
            P(("dp", "fsdp")),
            P(("dp", "fsdp")),
            P(("dp", "fsdp"), None),
            P(("dp", "fsdp")),
            P(("dp", "fsdp"), None),
            P(("dp", "fsdp")),
            P(),
            P(),
        ),
        check_vma=False,
    )
```

profile of v0, /device:TPU:0, one launch (start us, length us, event | category | flops | bytes accessed | tf_op | source)
XLA Modules:
  0.0 1603.0 jit_solution(9505542333634761871)
XLA Ops:
  19.4 42.7 %all-reduce.21 = (bf16[768]{0:T(1024)(128)(2,1)S(1)}, bf16[768]{0:T(1024)(128)(2,1)S(1)}, bf16[768]{0:T(1024)(128)(2,1)S(1)}, bf16[768]{0:T(1024)(128)(2,1)S(1)}...) all-reduce(bf16[768]{0:T(1024)(128)(2,1)S(1)} %dynamic-update-slice, ...), channel_id=1, replica_groups=mesh['dp'=4,'fsdp'=8] {'dp','fsdp'}, use_global_device_ids=true, to_apply=%add.3 | all-reduce | flops 9216 | bytes 36864
  72.0 15.1 multiply_reduce_fusion.7
  92.0 31.9 %convert_reduce_fusion.3 = bf16[26,38,768]{2,1,0:T(8,128)(2,1)} fusion(f32[26,38]{1,0:T(8,128)S(1)} %fusion.66, bf16[1,26,38,768]{3,2,1,0:T(8,128)(2,1)S(1)} %copy-done.35), kind=kLoop, calls=%fused_computation.120 | loop fusion | flops 2276352 | bytes 3039088 | tf_op jit(solution)/shard_map/convert_element_type | solution.py:215
  147.9 10.4 pad_reduce_fusion.1
  174.1 176.4 %while.33 = (s32[]{:T(128)}, bf16[2,588,768]{2,1,0:T(8,128)(2,1)}, f32[2,3,12,196]{3,2,1,0:T(8,128)S(1)}, bf16[2,3,196,768]{3,2,1,0:T(8,128)(2,1)}, bf16[768,230...) while((s32[]{:T(128)}, bf16[2,588,768]{2,1,0:T(8,128)(2,1)}, ...), condition=%wide.region_5.6_spmd, body=%wide.region_2.5_spmd.sunk | while | flops 2803264000 | bytes 120702992 | solution.py:179
  181.4 7.1 reshape.584
  207.1 7.9 fusion.195
  215.0 11.2 copy.348
  226.3 7.9 fusion.194
  234.2 11.4 copy.347
  245.6 7.0 fusion.196
  269.4 7.1 reshape.584
  295.0 7.9 fusion.195
  302.9 11.2 copy.348
  314.1 7.9 fusion.194
  322.1 11.4 copy.347
  333.5 7.0 fusion.196
  367.9 22.3 %fusion.89 = (f32[26,38]{1,0:T(8,128)S(1)}, f32[1,26,38,768]{3,0,2,1:T(1,128)S(1)}) fusion(f32[1,28,42,768]{3,0,2,1:T(1,128)S(1)} %bitcast.278, bf16[1,26,38,768]{3,2,1,0:T(8,128)(2,1)S(1)} %copy-done.26), kind=kLoop, calls=%fused_computation.182 | loop fusion | flops 2275364 | bytes 7591792 | tf_op jit(solution)/shard_map/reduce_sum | solution.py:22
  390.3 14.8 multiply_reduce_fusion.6
  405.7 30.8 %convert_reduce_fusion.4 = bf16[26,38,768]{2,1,0:T(8,128)(2,1)S(1)} fusion(f32[768]{0:T(1024)S(1)} %copy-done.68, f32[768]{0:T(1024)S(1)} %copy-done.56, f32[26,38]{1,0:T(8,128)S(1)} %add_rsqrt_fusion, f32[1,26,38,768]{3,0,2,1:T(1,128)S(1)} %get-tuple-element.407, f32[26,38]{1,0:T(8,128)S(1)} %broadcast_multiply_fusion.5), kind=kLoop, calls=%fused_computation.122 | loop fusion | flops 3793920 | bytes 4566752 | tf_op jit(solution)/shard_map/convert_element_type | solution.py:188
  437.0 10.7 fusion.93
  447.7 37.3 %convert_reduce_fusion = (f32[3072]{0:T(1024)}, bf16[988,3072]{1,0:T(8,128)(2,1)}, f32[988,3072]{1,0:T(8,128)S(1)}) fusion(f32[988,3072]{1,0:T(8,128)} %fusion.93, f32[3072]{0:T(1024)S(1)} %copy-done.62, bf16[988,768]{1,0:T(8,128)(2,1)S(1)} %copy-done.41, bf16[3072,768]{1,0:T(8,128)(2,1)} %all-gather.11.cloned.1.call-done), kind=kOutput, calls=%fused_computation.84 | convolution fusion | flops 4889601024 | bytes 36612096 | tf_op jit(solution)/shard_map/rd,fd->rf/dot_general | solution.py:220
  485.0 6.4 multiply_convert_fusion.1
  503.6 10.7 fusion.94
  520.5 35.1 %fusion.86 = (f32[26,38,768]{2,1,0:T(8,128)}, f32[26,38]{1,0:T(8,128)S(1)}) fusion(f32[26,38]{1,0:T(8,128)S(1)} %copy-done.53, f32[1,26,38,768]{3,0,2,1:T(1,128)S(1)} %copy-done.24, f32[26,38]{1,0:T(8,128)S(1)} %copy-done.49, f32[1,26,38,768]{3,0,2,1:T(1,128)} %reshape.561, f32[768]{0:T(1024)S(1)} %copy-done.57), kind=kLoop, calls=%fused_computation.180 | loop fusion | flops 3792932 | bytes 9120336 | tf_op jit(solution)/shard_map/mul | solution.py:24
  563.2 17.8 %convert_reduce_fusion.2 = (f32[768]{0:T(1024)}, f32[1,26,38,768]{3,0,2,1:T(1,128)S(1)}, bf16[1,26,38,768]{3,0,2,1:T(2,128)(2,1)}, f32[768]{0:T(1024)}) fusion(f32[26,38]{1,0:T(8,128)S(1)} %broadcast_multiply_fusion.4, f32[1,26,38,768]{3,0,2,1:T(1,128)S(1)} %copy-done.24, f32[26,38]{1,0:T(8,128)S(1)} %copy-done.49, f32[26,38]{1,0:T(8,128)S(1)} %div.59, ...), kind=kLoop, calls=%fused_computation.115 | loop fusion | flops 13656576 | bytes 15204656 | tf_op jit(solution)/shard_map/reduce_sum | solution.py:239
  584.7 10.4 pad_reduce_fusion
  600.5 487.0 %while.34 = (s32[]{:T(128)}, f32[768,2304]{1,0:T(8,128)}, f32[768]{0:T(1024)S(1)}, f32[768]{0:T(1024)S(1)}, f32[768,768]{1,0:T(8,128)}, /*index=5*/f32[196,196,6...) while((s32[]{:T(128)}, f32[768,2304]{1,0:T(8,128)}, ...), condition=%wide.region_15.16_spmd.clone, body=%wide.region_11.15_spmd.clone.sunk | while | flops 9613326336 | bytes 433143744 | solution.py:309
  617.4 9.2 reshape.588
  645.6 7.9 fusion.233
  653.5 11.2 copy.358
  664.7 8.0 fusion.232
  672.7 11.6 copy.357
  684.3 7.3 fusion.234
  722.8 8.0 copy.362
  730.7 8.3 fusion.237
  743.2 8.3 fusion.236
  767.7 8.9 convert_element_type.276
  786.0 32.3 %dynamic_update_slice.20 = f32[2,588,768]{2,0,1:T(2,128)} dynamic-update-slice(f32[2,588,768]{2,0,1:T(2,128)} %get-tuple-element.648, f32[1,588,768]{2,0,1:T(1,128)} %copy.367, s32[]{:T(128)S(6)} %copy.396, s32[]{:T(128)} %constant.61.clone.1..sunk, s32[]{:T(128)} %constant.61.clone.1..sunk) | dynamic-update-slice | bytes 3612676 | tf_op jit(solution)/shard_map/while/body/jit(dynamic_update_index_in_dim)/dynamic_update_slice | solution.py:309
  818.3 9.0 bitcast_add_fusion.8
  853.4 9.2 reshape.588
  881.6 7.9 fusion.233
  889.5 11.2 copy.358
  900.8 8.0 fusion.232
  908.8 11.6 copy.357
  920.4 7.3 fusion.234
  958.9 8.0 copy.362
  966.9 8.3 fusion.237
  979.6 8.3 fusion.236
  1004.1 8.6 convert_element_type.276
  1022.1 32.3 %dynamic_update_slice.20 = f32[2,588,768]{2,0,1:T(2,128)} dynamic-update-slice(f32[2,588,768]{2,0,1:T(2,128)} %get-tuple-element.648, f32[1,588,768]{2,0,1:T(1,128)} %copy.367, s32[]{:T(128)S(6)} %copy.396, s32[]{:T(128)} %constant.61.clone.1..sunk, s32[]{:T(128)} %constant.61.clone.1..sunk) | dynamic-update-slice | bytes 3612676 | tf_op jit(solution)/shard_map/while/body/jit(dynamic_update_index_in_dim)/dynamic_update_slice | solution.py:309
  1054.4 12.7 bitcast_add_fusion.8
  1071.4 7.3 select_add_fusion.7
  1088.9 10.1 fusion.96
  1100.4 10.3 fusion.95
  1117.8 28.1 %multiply_reduce_fusion.3 = (f32[768]{0:T(1024)S(1)}, f32[26,38]{1,0:T(8,128)S(1)}, f32[26,38]{1,0:T(8,128)S(1)}, f32[768]{0:T(1024)S(1)}) fusion(f32[1,28,42,768]{3,0,2,1:T(1,128)S(1)} %bitcast.275, f32[26,38]{1,0:T(8,128)S(1)} %copy-done.51, f32[26,38]{1,0:T(8,128)S(1)} %copy-done.47, bf16[1,26,38,768]{3,2,1,0:T(8,128)(2,1)S(1)} %copy-done.27, ...), kind=kLoop, calls=%fused_computation.114 | loop fusion | flops 7584328 | bytes 4577728 | tf_op jit(solution)/shard_map/reduce_sum | solution.py:312
  1146.0 9.8 add_convert_fusion.3
  1157.2 16.6 %copy.225 = f32[196,196,64]{0,2,1:T(8,128)} copy(f32[196,196,64]{1,2,0:T(8,128)} %get-tuple-element.731) | data formatting | bytes 19668992 | tf_op jit(solution)/shard_map/while | solution.py:309
  1173.9 10.7 convolution_bitcast_fusion.1
  1184.7 7.1 convolution_bitcast_fusion.2
  1191.8 42.3 %all-reduce.20 = (f32[768]{0:T(1024)S(1)}, f32[768]{0:T(1024)S(1)}, f32[768]{0:T(1024)S(1)}, f32[768]{0:T(1024)S(1)}, f32[768]{0:T(1024)S(1)}, /*index=5*/f32[76...) all-reduce(f32[768]{0:T(1024)S(1)} %get-tuple-element.728, ...), channel_id=3, replica_groups=mesh['dp'=4,'fsdp'=8] {'dp','fsdp'}, use_global_device_ids=true, to_apply=%region_19.20.clone | all-reduce | flops 12672 | bytes 101376
  1239.4 73.3 %reduce-scatter.5.cloned.1.call-done = f32[24,2304]{1,0:T(8,128)} async-done(((f32[768,2304]{1,0:T(8,128)}), f32[24,2304]{1,0:T(8,128)}) %reduce-scatter.5.cloned.1.call-update) | async-done | bytes 221200 | tf_op jit(solution)/shard_map/reduce_scatter | solution.py:322
  1312.6 141.4 %reduce-scatter.11.cloned.1.call-done = f32[96,768]{1,0:T(8,128)} async-done(((f32[3072,768]{1,0:T(8,128)}), f32[96,768]{1,0:T(8,128)}) %reduce-scatter.11.cloned.1.call-update) | async-done | bytes 294928 | tf_op jit(solution)/shard_map/reduce_scatter | solution.py:333
  1454.0 142.0 %reduce-scatter.9.cloned.1.call-done = f32[24,3072]{1,0:T(8,128)} async-done(((f32[768,3072]{1,0:T(8,128)}), f32[24,3072]{1,0:T(8,128)}) %reduce-scatter.9.cloned.1.call-update) | async-done | bytes 294928 | tf_op jit(solution)/shard_map/reduce_scatter | solution.py:331
  (425 shorter events, 412.2 us)
Async XLA Ops:
  7.2 157.7 %copy-start = (bf16[27,64]{1,0:T(8,128)(2,1)S(1)}, bf16[27,64]{1,0:T(8,128)(2,1)}, u32[]{:S(2)}) copy-start(bf16[27,64]{1,0:T(8,128)(2,1)} %param.45) | copy-start | bytes 10372
  7.2 64.8 %copy-start.25 = (bf16[1,26,38,768]{3,2,1,0:T(8,128)(2,1)S(1)}, bf16[1,26,38,768]{3,2,1,0:T(8,128)(2,1)}, u32[]{:S(2)}) copy-start(bf16[1,26,38,768]{3,2,1,0:T(8,128)(2,1)} %param.25) | copy-start | bytes 4552708
  7.2 84.8 %copy-start.35 = (bf16[1,26,38,768]{3,2,1,0:T(8,128)(2,1)S(1)}, bf16[1,26,38,768]{3,2,1,0:T(8,128)(2,1)}, u32[]{:S(2)}) copy-start(bf16[1,26,38,768]{3,2,1,0:T(8,128)(2,1)} %param.26) | copy-start | bytes 4552708
  7.2 166.9 %all-gather.5.cloned.1.call-start = ((), (), s32[]{:S(2)}) async-start(), calls=%async_computation.4 | async-start | bytes 3649536 | tf_op jit(solution)/shard_map/all_gather | solution.py:130
  8.0 344.5 %all-gather.7.cloned.1.call-start = ((), (), s32[]{:S(2)}) async-start(), calls=%async_computation.5 | async-start | bytes 1216512 | tf_op jit(solution)/shard_map/all_gather | solution.py:133
  8.7 428.3 %all-gather.9.cloned.1.call-start = ((), (), s32[]{:S(2)}) async-start(), calls=%async_computation.6 | async-start | bytes 4866048 | tf_op jit(solution)/shard_map/all_gather | solution.py:139
  9.4 438.3 %all-gather.11.cloned.1.call-start = ((), (), s32[]{:S(2)}) async-start(), calls=%async_computation.7 | async-start | bytes 4866048 | tf_op jit(solution)/shard_map/all_gather | solution.py:141
  10.0 1229.3 %reduce-scatter.7.cloned.1.call-start = ((), (), s32[]{:S(2)}) async-start(), calls=%async_computation.9 | async-start | bytes 2433024 | tf_op jit(solution)/shard_map/reduce_scatter | solution.py:325
  62.1 25.0 %copy-start.76 = (s32[196]{0:T(256)S(1)}, s32[196]{0:T(256)}, u32[]{:S(2)}) copy-start(s32[196]{0:T(256)} %and_select_fusion) | copy-start | bytes 2356
  62.1 25.1 %copy-start.75 = (s32[196]{0:T(256)S(1)}, s32[196]{0:T(256)}, u32[]{:S(2)}) copy-start(s32[196]{0:T(256)} %and_select_fusion.1) | copy-start | bytes 2356
  62.1 25.9 %copy-start.79 = (s32[1,300]{1,0:T(1,128)S(1)}, s32[1,300]{1,0:T(1,128)}, u32[]{:S(2)}) copy-start(s32[1,300]{1,0:T(1,128)} %param.29) | copy-start | bytes 3604
  63.3 78.1 %copy-start.60 = (f32[768]{0:T(1024)}, f32[768]{0:T(1024)S(1)}, u32[]{:S(2)}) copy-start(f32[768]{0:T(1024)S(1)} %convert_element_type.145) | copy-start | bytes 9220
  72.0 69.5 %copy-start.46 = (f32[26,38]{1,0:T(8,128)}, f32[26,38]{1,0:T(8,128)S(1)}, u32[]{:S(2)}) copy-start(f32[26,38]{1,0:T(8,128)S(1)} %broadcast_multiply_fusion.6) | copy-start | bytes 11860
  87.1 54.4 %copy-start.50 = (f32[26,38]{1,0:T(8,128)}, f32[26,38]{1,0:T(8,128)S(1)}, u32[]{:S(2)}) copy-start(f32[26,38]{1,0:T(8,128)S(1)} %add_rsqrt_fusion.1) | copy-start | bytes 11860
  87.2 47.4 %copy-start.38 = (s32[196,196]{0,1:T(8,128)}, s32[196,196]{0,1:T(8,128)S(1)}, u32[]{:S(2)}) copy-start(s32[196,196]{0,1:T(8,128)S(1)} %subtract_add_fusion) | copy-start | bytes 460996
  234.2 11.4 copy-start.20
  234.2 11.4 copy-start.21
  322.1 11.4 copy-start.20
  322.1 11.4 copy-start.21
  350.5 6.6 copy-start.45
  350.6 6.6 copy-start.71
  361.9 6.0 copy-start.26
  390.2 14.9 copy-start.23
  390.2 15.5 copy-start.56
  390.2 15.5 copy-start.68
  390.2 14.9 copy-start.48
  436.9 10.8 copy-start.43
  436.9 10.8 copy-start.41
  436.9 10.8 copy-start.62
  485.0 9.0 copy-start.77
  485.0 9.0 copy-start.80
  514.3 6.2 copy-start.24
  514.3 6.2 copy-start.49
  514.3 6.2 copy-start.53
  514.3 6.2 copy-start.57
  605.6 5.9 copy-start.15
  632.4 32.3 %copy-start.4 = (bf16[3,196,12,64]{3,2,1,0:T(8,128)(2,1)}, bf16[3,196,12,64]{3,2,1,0:T(8,128)(2,1)S(1)}, u32[]{:S(2)}) copy-start(bf16[3,196,12,64]{3,2,1,0:T(8,128)(2,1)S(1)} %get-tuple-element.588) | copy-start | bytes 2709508 | tf_op jit(solution)/shard_map/while
  672.7 11.6 copy-start.10
  672.7 11.6 copy-start.12
  684.3 7.3 copy-start.9
  699.9 8.5 slice-start
  782.9 35.4 %copy-start.5 = (bf16[3,196,12,64]{3,2,1,0:T(8,128)(2,1)S(1)}, bf16[3,196,12,64]{3,2,1,0:T(8,128)(2,1)}, u32[]{:S(2)}) copy-start(bf16[3,196,12,64]{3,2,1,0:T(8,128)(2,1)} %copy-done.4) | copy-start | bytes 2709508 | tf_op jit(solution)/shard_map/while
  868.4 32.3 %copy-start.4 = (bf16[3,196,12,64]{3,2,1,0:T(8,128)(2,1)}, bf16[3,196,12,64]{3,2,1,0:T(8,128)(2,1)S(1)}, u32[]{:S(2)}) copy-start(bf16[3,196,12,64]{3,2,1,0:T(8,128)(2,1)S(1)} %get-tuple-element.588) | copy-start | bytes 2709508 | tf_op jit(solution)/shard_map/while
  908.8 11.6 copy-start.10
  908.8 11.7 copy-start.12
  920.4 7.3 copy-start.9
  936.1 8.5 slice-start
  1019.0 35.4 %copy-start.5 = (bf16[3,196,12,64]{3,2,1,0:T(8,128)(2,1)S(1)}, bf16[3,196,12,64]{3,2,1,0:T(8,128)(2,1)}, u32[]{:S(2)}) copy-start(bf16[3,196,12,64]{3,2,1,0:T(8,128)(2,1)} %copy-done.4) | copy-start | bytes 2709508 | tf_op jit(solution)/shard_map/while
  1071.4 7.3 copy-start.31
  1071.4 7.3 copy-start.73
  1071.4 7.3 copy-start.82
  1087.5 225.2 %reduce-scatter.5.cloned.1.call-start = ((), (), s32[]{:S(2)}) async-start(), calls=%async_computation.8 | async-start | bytes 7299072 | tf_op jit(solution)/shard_map/reduce_scatter | solution.py:322
  1088.0 366.0 %reduce-scatter.11.cloned.1.call-start = ((), (), s32[]{:S(2)}) async-start(), calls=%async_computation.11 | async-start | bytes 9732096 | tf_op jit(solution)/shard_map/reduce_scatter | solution.py:333
  1099.0 497.0 %reduce-scatter.9.cloned.1.call-start = ((), (), s32[]{:S(2)}) async-start(), calls=%async_computation.10 | async-start | bytes 9732096 | tf_op jit(solution)/shard_map/reduce_scatter | solution.py:331
  1117.8 28.2 %copy-start.29 = (f32[1,26,38,768]{3,0,2,1:T(1,128)S(1)}, f32[1,26,38,768]{3,0,2,1:T(1,128)}, u32[]{:S(2)}) copy-start(f32[1,26,38,768]{3,0,2,1:T(1,128)} %copy-done.28) | copy-start | bytes 9105412
  1157.2 16.6 %copy-start.39 = (s32[196,196]{0,1:T(8,128)S(1)}, s32[196,196]{0,1:T(8,128)}, u32[]{:S(2)}) copy-start(s32[196,196]{0,1:T(8,128)} %copy-done.38) | copy-start | bytes 460996
  1173.9 10.7 copy-start.22
  1173.9 10.7 copy-start.40
  1184.6 7.2 copy-start.63
  1184.6 7.2 copy-start.64
  1184.6 7.2 copy-start.65
  1184.6 7.2 copy-start.66
  1184.7 7.2 copy-start.70
  1184.7 411.3 %copy-start.1 = (bf16[27,64]{1,0:T(8,128)(2,1)S(1)}, bf16[27,64]{1,0:T(8,128)(2,1)}, u32[]{:S(2)}) copy-start(bf16[27,64]{1,0:T(8,128)(2,1)} %param.45) | copy-start | bytes 10372
  (55 other events, 186.1 us)
Sparse Core Ops, SparseCore 0:
  11.1 63.4 all-gather.4
  77.5 52.9 all-gather.6
  133.5 62.6 all-gather.8
  199.0 62.4 all-gather.10
  1087.6 99.8 reduce-scatter.6
  1194.5 118.0 reduce-scatter.4
  1319.1 134.8 reduce-scatter.10
  1461.5 134.4 reduce-scatter.8
where the time goes:
time: 1620 us; the launch traced here: 1600 us
  local copies, waits for them, and re-layouts  515 us (32%)
  waiting for transfers between devices  360 us (22%)
  matrix products  357 us (22%)
  other arithmetic  259 us (16%)
  blocking collectives  85 us (5%)
  between operations  16.5 us (1%)
    reduce_scatter x1, waiting for transfers between devices, local(): lax.psum_scatter(up_weight_grad, ('dp', 'fsdp'), scatter_dimension=0, til...  142 us
    reduce_scatter x1, waiting for transfers between devices, local(): lax.psum_scatter(down_weight_grad, ('dp', 'fsdp'), scatter_dimension=0, t...  141 us
    unnamed x2, blocking collectives  85 us
    reduce_scatter x1, waiting for transfers between devices, local(): lax.psum_scatter(in_weight_grad, ('dp', 'fsdp'), scatter_dimension=0, til...  73.3 us
    dynamic_update_slice x4, local copies, waits for them, and re-layouts, local(): lax.scan(backward_block, start, (blocks, log_totals, branch_blocks))  70.8 us
    while x116, local copies, waits for them, and re-layouts  67 us
    dot_general x4, local copies, waits for them, and re-layouts, score_block(): jnp.einsum('wqhc,qkc->whqk', queries, cols_low, preferred_element_type=jn...  46 us
    dot_general x4, local copies, waits for them, and re-layouts, score_block(): jnp.einsum('wqhc,qkc->whqk', queries, rows_low, preferred_element_type=jn...  44.9 us
  transfers between devices with their start and end apart: 8, of which 3 were waited for; matrix products, arithmetic and copies ran while one was open for 31% of the time, Pallas kernels for 0%

commit v1 on v0

v1 whole, which is shorter than its diff:
```python
import jax
import jax.numpy as jnp
import numpy as np
from jax import lax
from jax.experimental import pallas as pl
from jax.experimental.pallas import tpu as pltpu
from jax.sharding import PartitionSpec as P

D = 768
HEADS = 12
HD = 64
FF = 3072
WIN = 14
GH = 26
GW = 38
NBOX = 300
ACROSS = 3
WINDOWS = 6
LINE = 16
TOK = WIN * LINE
REAL = GH * GW
DENSE = 992
PAIRS = HEADS // 2
STARTS = (0, 14, 28)
WIDTHS = (14, 14, 10)
CHUNK = 512
SPLITS = ((0, 256), (256, 256), (512, 256), (768, 224))
epsilon = 1e-06
f32 = jnp.float32
bf16 = jnp.bfloat16
LIMIT = 60 * 1024 * 1024


def dot(a, b):
    return lax.dot_general(a, b, (((1,), (0,)), ((), ())), preferred_element_type=f32)


def dot_bt(a, b):
    return lax.dot_general(a, b, (((1,), (1,)), ((), ())), preferred_element_type=f32)


def dot_at(a, b):
    return lax.dot_general(a, b, (((0,), (0,)), ((), ())), preferred_element_type=f32)


def unit_of(x):
    center = x - jnp.mean(x, axis=-1, keepdims=True)
    inverse = lax.rsqrt(jnp.mean(center * center, axis=-1, keepdims=True) + epsilon)
    return center * inverse, inverse


def norm_back(grad, unit, inverse, gain):
    scaled = grad * gain
    return inverse * (
        scaled
        - jnp.mean(scaled, axis=-1, keepdims=True)
        - unit * jnp.mean(scaled * unit, axis=-1, keepdims=True)
    )


def place_of(row):
    return (row // WIN) * ACROSS, row % WIN


def spread_row(row, value, out_ref):
    first, place = place_of(row)
    for piece, (start, width) in enumerate(zip(STARTS, WIDTHS)):
        part = value[start : start + width]
        part = jnp.concatenate([part, jnp.zeros((LINE - width, part.shape[1]), part.dtype)], axis=0)
        out_ref[(first + piece) * WIN + place] = part.astype(out_ref.dtype)


def join_row(row, in_ref):
    first, place = place_of(row)
    return jnp.concatenate(
        [
            in_ref[(first + piece) * WIN + place].astype(f32)[:width]
            for piece, width in enumerate(WIDTHS)
        ],
        axis=0,
    )


def begin_kernel(img_ref, vec_ref, tiles_ref):
    tiles_ref[...] = jnp.zeros_like(tiles_ref)
    gain = vec_ref[0:1, :]
    shift = vec_ref[1:2, :]
    for row in range(GH):
        unit, _ = unit_of(img_ref[row].astype(f32))
        spread_row(row, unit * gain + shift, tiles_ref)


def weight_kernel(count_ref, grad_ref, rows_ref, cols_ref, valid_ref, cot_ref, upd_ref):
    slot = lax.broadcasted_iota(jnp.int32, (NBOX, 1), 0)
    live = (slot < count_ref[0]) & (valid_ref[...] == 1)
    rows = rows_ref[...]
    cols = cols_ref[...]
    top = jnp.minimum(rows[:, 0:1], rows[:, 1:2])
    low = jnp.maximum(rows[:, 0:1], rows[:, 1:2])
    left = jnp.minimum(cols[:, 0:1], cols[:, 1:2])
    right = jnp.maximum(cols[:, 0:1], cols[:, 1:2])
    grid_r = lax.broadcasted_iota(jnp.int32, (NBOX, GH), 1)
    grid_c = lax.broadcasted_iota(jnp.int32, (NBOX, GW), 1)
    in_rows = jnp.where((grid_r >= top) & (grid_r < low) & live, 1.0, 0.0)
    in_cols = jnp.where((grid_c >= left) & (grid_c < right), 1.0, 0.0)
    inside = dot_at(in_cols.astype(bf16), in_rows.astype(bf16))
    total = jnp.sum(jnp.where(live, 1.0, 0.0))
    weight = 1.0 + 2.0 * inside / jnp.maximum(total, 1.0)
    for row in range(GH):
        cot_ref[row * GW : (row + 1) * GW, :] = grad_ref[row].astype(f32) * weight[:, row : row + 1]
    cot_ref[REAL:, :] = jnp.zeros((DENSE - REAL, D), f32)
    upd_ref[...] = cot_ref[...].astype(bf16)


def lane_iota(shape):
    return lax.broadcasted_iota(jnp.int32, shape, len(shape) - 1)


def position_terms(queries, table):
    both = dot(queries, table)
    row_part = both[:, :128].reshape(WIN, LINE, 128)
    col_part = both[:, 128:].reshape(WIN, LINE, 128)
    lane = lane_iota((LINE, 128))
    local = lane % 32
    out = []
    for place in range(WIN):
        rolled_r = pltpu.roll(row_part[place], (place - 13) % 128, 1)
        rolled_c = pltpu.roll(col_part[place], 0, 1, stride=1, stride_axis=0)
        value = jnp.where(local < 16, rolled_r, rolled_c)
        high = value.astype(bf16).astype(f32)
        value = jnp.where(lane < 64, high, value - high)
        value = jnp.where(lane == 14, 1.0, value)
        out.append(value)
    return jnp.concatenate(out, axis=0).astype(bf16)


def keep_head(value, head):
    lane = lane_iota(value.shape)
    return jnp.where((lane < HD) == (head == 0), value, jnp.zeros_like(value))


def forward_kernel(
    tiles_ref, weight_ref, bias_ref, out_w_ref, out_b_ref, table_ref, hot_ref, packed_ref, soft_ref, att_ref, branch_ref
):
    packed_ref[...] = (dot(tiles_ref[...], weight_ref[...]) + bias_ref[...]).astype(bf16)
    for pair in range(PAIRS):
        at = pair * 128
        queries = packed_ref[:, at : at + 128]
        keys = packed_ref[:, D + at : D + at + 128]
        values = packed_ref[:, 2 * D + at : 2 * D + at + 128]
        left = jnp.concatenate([queries, position_terms(queries, table_ref[...])], axis=1)
        parts = []
        for head in range(2):
            scaled = (keep_head(keys.astype(f32), head) * 0.125).astype(bf16)
            right = jnp.concatenate([scaled, hot_ref[head]], axis=1)
            scores = dot_bt(left, right)
            power = jnp.exp(scores - jnp.max(scores, axis=-1, keepdims=True))
            soft = (power * (1.0 / jnp.sum(power, axis=-1, keepdims=True))).astype(bf16)
            soft_ref[2 * pair + head] = soft
            parts.append(dot(soft, values))
        lane = lane_iota((TOK, 128))
        att_ref[:, at : at + 128] = jnp.where(lane < HD, parts[0], parts[1]).astype(bf16)
    branch_ref[...] = dot(att_ref[...], out_w_ref[...]) + out_b_ref[...]


def backward_kernel(
    packed_ref,
    soft_ref,
    att_ref,
    gbr_ref,
    tiles_ref,
    out_w_ref,
    table_ref,
    hot_ref,
    gpacked_ref,
    gin_ref,
    gout_ref,
    gbias_ref,
    gtab_ref,
    att_all,
    gbr_all,
    gpacked_all,
    gatt_ref,
):
    step = pl.program_id(0)

    @pl.when(step == 0)
    def _():
        gbias_ref[...] = jnp.zeros_like(gbias_ref)
        gtab_ref[...] = jnp.zeros_like(gtab_ref)

    gatt_ref[...] = dot_bt(gbr_ref[...], out_w_ref[...]).astype(bf16)
    lane = lane_iota((LINE, 128))
    local = lane % 32
    wide = lane_iota((TOK, 128))
    for pair in range(PAIRS):
        at = pair * 128
        queries = packed_ref[:, at : at + 128]
        keys = packed_ref[:, D + at : D + at + 128]
        values = packed_ref[:, 2 * D + at : 2 * D + at + 128]
        gatt = gatt_ref[:, at : at + 128]
        product = gatt.astype(f32) * att_ref[:, at : at + 128].astype(f32)
        left = []
        right = []
        gvalues = []
        gkeys = []
        for head in range(2):
            soft = soft_ref[2 * pair + head]
            delta = jnp.sum(keep_head(product, head), axis=-1, keepdims=True)
            gprobs = dot_bt(gatt, keep_head(values.astype(f32), head).astype(bf16))
            gscores = (soft.astype(f32) * (gprobs - delta)).astype(bf16)
            scaled = (keep_head(keys.astype(f32), head) * 0.125).astype(bf16)
            left.append(gscores)
            right.append(jnp.concatenate([scaled, hot_ref[head]], axis=1))
            gvalues.append(dot_at(soft, gatt))
            gkeys.append(dot_at(gscores, queries))
        both = dot(left[0], right[0]) + dot(left[1], right[1])
        terms = both[:, 128:].reshape(WIN, LINE, 128)
        rolled = []
        for place in range(WIN):
            value = terms[place]
            high = value.astype(bf16).astype(f32)
            value = jnp.where(lane < 64, high, value - high)
            row_part = jnp.where(local < WIN, value, 0.0)
            col_part = jnp.where((local >= 16) & (local < 16 + WIN), value, 0.0)
            row_part = pltpu.roll(row_part, 13 - place, 1)
            col_part = pltpu.roll(col_part, 0, 1, stride=1, stride_axis=0)
            rolled.append(jnp.concatenate([row_part, col_part], axis=1))
        rolled = jnp.concatenate(rolled, axis=0).astype(bf16)
        gqueries = both[:, :128] + dot_bt(rolled, table_ref[...])
        gtab_ref[...] += dot_at(rolled, queries)
        gq = gqueries.astype(bf16)
        gk = (jnp.where(wide < HD, gkeys[0], gkeys[1]) * 0.125).astype(bf16)
        gv = jnp.where(wide < HD, gvalues[0], gvalues[1]).astype(bf16)
        gpacked_ref[:, at : at + 128] = gq
        gpacked_ref[:, D + at : D + at + 128] = gk
        gpacked_ref[:, 2 * D + at : 2 * D + at + 128] = gv
        gbias_ref[0:1, at : at + 128] += jnp.sum(gq.astype(f32), axis=0, keepdims=True)
        gbias_ref[1:2, at : at + 128] += jnp.sum(gv.astype(f32), axis=0, keepdims=True)
    here = pl.ds(pl.multiple_of(step * TOK, TOK), TOK)
    att_all[here, :] = att_ref[...]
    gbr_all[here, :] = gbr_ref[...]
    gpacked_all[here, :] = gpacked_ref[...]

    @pl.when(step == WINDOWS - 1)
    def _():
        gout_ref[...] = dot_at(att_all[...], gbr_all[...]).astype(bf16)
        for part in range(0, 3 * D, D):
            gin_ref[:, part : part + D] = dot_at(tiles_ref[...], gpacked_all[:, part : part + D]).astype(bf16)


def gelu_parts(hidden):
    size = jnp.abs(hidden)
    power = jnp.exp(hidden * hidden * -0.5)
    denominator = 1.0 + (0.3275911 * 0.7071067811865476) * size
    near = pl.reciprocal(denominator, approx=True)
    near = near * (2.0 - denominator * near)
    series = near * (
        0.254829592
        + near * (-0.284496736 + near * (1.421413741 + near * (-1.453152027 + near * 1.061405429)))
    )
    tail = 0.5 * series * power
    normal = jnp.where(hidden >= 0, 1.0 - tail, tail)
    return hidden * normal, normal + hidden * power * 0.3989422804014327


def middle_kernel(
    img_ref,
    branch_ref,
    cot_ref,
    gupd_ref,
    vec_ref,
    up_ref,
    upb_ref,
    down_ref,
    out_ref,
    gbr_ref,
    gup_ref,
    gdown_ref,
    gupb_ref,
    sums_ref,
    mid,
    normed,
    update,
    gnorm,
    active,
    ghidden,
):
    step = pl.program_id(0)
    gain = vec_ref[2:3, :]
    shift = vec_ref[3:4, :]

    @pl.when(step == 0)
    def _():
        for row in range(GH):
            mid[row * GW : (row + 1) * GW, :] = img_ref[row].astype(f32) + join_row(row, branch_ref)
        mid[REAL:, :] = jnp.zeros((DENSE - REAL, D), f32)
        update[...] = jnp.zeros_like(update)
        gnorm[...] = jnp.zeros_like(gnorm)

        def chunk(index, carry):
            here = pl.ds(pl.multiple_of(index * 32, 32), 32)
            unit, _ = unit_of(mid[here, :])
            normed[here, :] = (unit * gain + shift).astype(bf16)
            return carry

        lax.fori_loop(0, DENSE // 32, chunk, 0)

    for start, size in SPLITS:
        here = slice(start, start + size)
        hidden = dot(normed[here, :], up_ref[...]) + upb_ref[...]
        gactive = dot_bt(gupd_ref[here, :], down_ref[...])
        act, slope = gelu_parts(hidden)
        act = act.astype(bf16)
        gh = (gactive * slope).astype(bf16)
        active[here, :] = act
        ghidden[here, :] = gh
        update[here, :] += dot(act, down_ref[...])
        gnorm[here, :] += dot_bt(gh, up_ref[...])
    gupb_ref[...] = jnp.sum(ghidden[...].astype(f32), axis=0, keepdims=True)
    gdown_ref[...] = dot_at(active[...], gupd_ref[...]).astype(bf16)
    gup_ref[...] = dot_at(normed[...], ghidden[...]).astype(bf16)

    @pl.when(step == pl.num_programs(0) - 1)
    def _():
        down_bias = vec_ref[4:5, :]
        for row in range(GH):
            here = slice(row * GW, (row + 1) * GW)
            out_ref[row] = (mid[here, :] + update[here, :] + down_bias).astype(bf16)

        def chunk(index, carry):
            here = pl.ds(pl.multiple_of(index * 32, 32), 32)
            unit, inverse = unit_of(mid[here, :])
            grad = gnorm[here, :]
            cot = cot_ref[here, :]
            result = cot + norm_back(grad, unit, inverse, gain)
            rounded = result.astype(bf16).astype(f32)
            update[here, :] = rounded
            gain_sum, shift_sum, branch_sum, bias_sum = carry
            return (
                gain_sum + jnp.sum((grad * unit).reshape(4, 8, D), axis=0),
                shift_sum + jnp.sum(grad.reshape(4, 8, D), axis=0),
                branch_sum + jnp.sum(rounded.reshape(4, 8, D), axis=0),
                bias_sum + jnp.sum(cot.astype(bf16).astype(f32).reshape(4, 8, D), axis=0),
            )

        zero = jnp.zeros((8, D), f32)
        sums = lax.fori_loop(0, DENSE // 32, chunk, (zero,) * 4)
        sums_ref[...] = jnp.concatenate(
            [jnp.sum(s, axis=0, keepdims=True) for s in sums] + [jnp.zeros((4, D), f32)], axis=0
        )
        gbr_ref[...] = jnp.zeros_like(gbr_ref)
        for row in range(GH):
            spread_row(row, update[row * GW : (row + 1) * GW, :], gbr_ref)


def end_kernel(img_ref, gbr_ref, gpacked_ref, weight_ref, vec_ref, out_ref, sums_ref, gtiles):
    gain = vec_ref[0:1, :]
    for window in range(WINDOWS):
        value = dot_bt(gpacked_ref[window * TOK : (window + 1) * TOK, :], weight_ref[...])
        gtiles[window * WIN : (window + 1) * WIN] = value.reshape(WIN, LINE, D)
    gain_sum = jnp.zeros((1, D), f32)
    shift_sum = jnp.zeros((1, D), f32)
    for row in range(GH):
        unit, inverse = unit_of(img_ref[row].astype(f32))
        grad = join_row(row, gtiles)
        gain_sum += jnp.sum(grad * unit, axis=0, keepdims=True)
        shift_sum += jnp.sum(grad, axis=0, keepdims=True)
        out_ref[row] = (join_row(row, gbr_ref) + norm_back(grad, unit, inverse, gain)).astype(bf16)
    sums_ref[...] = jnp.concatenate([gain_sum, shift_sum, jnp.zeros((6, D), f32)], axis=0)


def params(steps=0):
    return pltpu.CompilerParams(
        vmem_limit_bytes=LIMIT, dimension_semantics=("arbitrary",) * steps if steps else None
    )


VMEM = pl.BlockSpec(memory_space=pltpu.VMEM)
SMEM = pl.BlockSpec(memory_space=pltpu.SMEM)


def whole(shape):
    return pl.BlockSpec(shape, lambda i: (0,) * len(shape))


def shaped(shape, dtype):
    return jax.ShapeDtypeStruct(shape, dtype)


def begin(images, vectors):
    return pl.pallas_call(
        begin_kernel,
        out_shape=shaped((WINDOWS * WIN, LINE, D), bf16),
        in_specs=[VMEM, VMEM],
        out_specs=VMEM,
        compiler_params=params(),
        cost_estimate=pl.CostEstimate(flops=30_000_000, bytes_accessed=4_000_000, transcendentals=0),
        name="begin",
    )(images, vectors)


def weigh(count, grad_out, rows, cols, valid):
    return pl.pallas_call(
        weight_kernel,
        out_shape=(shaped((DENSE, D), f32), shaped((DENSE, D), bf16)),
        in_specs=[SMEM] + [VMEM] * 4,
        out_specs=(VMEM, VMEM),
        compiler_params=params(),
        cost_estimate=pl.CostEstimate(flops=30_000_000, bytes_accessed=6_000_000, transcendentals=0),
        name="weigh",
    )(count, grad_out, rows, cols, valid)


def forward(tiles, weight, bias, out_w, out_b, table, hot):
    per = lambda *shape: pl.BlockSpec(shape, lambda i: (i,) + (0,) * (len(shape) - 1))
    return pl.pallas_call(
        forward_kernel,
        grid=(WINDOWS,),
        out_shape=(
            shaped((WINDOWS * TOK, 3 * D), bf16),
            shaped((WINDOWS * HEADS, TOK, TOK), bf16),
            shaped((WINDOWS * TOK, D), bf16),
            shaped((WINDOWS * TOK, D), f32),
        ),
        in_specs=[
            per(TOK, D),
            whole((D, 3 * D)),
            whole((1, 3 * D)),
            whole((D, D)),
            whole((1, D)),
            whole((128, 256)),
            whole((2, TOK, 128)),
        ],
        out_specs=(per(TOK, 3 * D), per(HEADS, TOK, TOK), per(TOK, D), per(TOK, D)),
        compiler_params=params(1),
        cost_estimate=pl.CostEstimate(flops=9_000_000_000, bytes_accessed=25_000_000, transcendentals=4_000_000),
        name="attend",
    )(tiles, weight, bias, out_w, out_b, table, hot)


def middle(images, branch, cot, gupd, vectors, up, up_bias, down):
    return pl.pallas_call(
        middle_kernel,
        grid=(FF // CHUNK,),
        out_shape=(
            shaped((GH, GW, D), bf16),
            shaped((WINDOWS * WIN, LINE, D), bf16),
            shaped((D, FF), bf16),
            shaped((FF, D), bf16),
            shaped((1, FF), f32),
            shaped((8, D), f32),
        ),
        in_specs=[
            whole((GH, GW, D)),
            whole((WINDOWS * WIN, LINE, D)),
            whole((DENSE, D)),
            whole((DENSE, D)),
            whole((8, D)),
            pl.BlockSpec((D, CHUNK), lambda i: (0, i)),
            pl.BlockSpec((1, CHUNK), lambda i: (0, i)),
            pl.BlockSpec((CHUNK, D), lambda i: (i, 0)),
        ],
        out_specs=(
            whole((GH, GW, D)),
            whole((WINDOWS * WIN, LINE, D)),
            pl.BlockSpec((D, CHUNK), lambda i: (0, i)),
            pl.BlockSpec((CHUNK, D), lambda i: (i, 0)),
            pl.BlockSpec((1, CHUNK), lambda i: (0, i)),
            whole((8, D)),
        ),
        scratch_shapes=[
            pltpu.VMEM((DENSE, D), f32),
            pltpu.VMEM((DENSE, D), bf16),
            pltpu.VMEM((DENSE, D), f32),
            pltpu.VMEM((DENSE, D), f32),
            pltpu.VMEM((DENSE, CHUNK), bf16),
            pltpu.VMEM((DENSE, CHUNK), bf16),
        ],
        compiler_params=params(1),
        cost_estimate=pl.CostEstimate(flops=28_000_000_000, bytes_accessed=36_000_000, transcendentals=6_000_000),
        name="feed",
    )(images, branch, cot, gupd, vectors, up, up_bias, down)


def backward(packed, soft, att, gbr, tiles, out_w, table, hot):
    per = lambda *shape: pl.BlockSpec(shape, lambda i: (i,) + (0,) * (len(shape) - 1))
    return pl.pallas_call(
        backward_kernel,
        grid=(WINDOWS,),
        out_shape=(
            shaped((WINDOWS * TOK, 3 * D), bf16),
            shaped((D, 3 * D), bf16),
            shaped((D, D), bf16),
            shaped((8, D), f32),
            shaped((256, 128), f32),
        ),
        in_specs=[
            per(TOK, 3 * D),
            per(HEADS, TOK, TOK),
            per(TOK, D),
            per(TOK, D),
            whole((WINDOWS * TOK, D)),
            whole((D, D)),
            whole((128, 256)),
            whole((2, TOK, 128)),
        ],
        out_specs=(per(TOK, 3 * D), whole((D, 3 * D)), whole((D, D)), whole((8, D)), whole((256, 128))),
        scratch_shapes=[
            pltpu.VMEM((WINDOWS * TOK, D), bf16),
            pltpu.VMEM((WINDOWS * TOK, D), bf16),
            pltpu.VMEM((WINDOWS * TOK, 3 * D), bf16),
            pltpu.VMEM((TOK, D), bf16),
        ],
        compiler_params=params(1),
        cost_estimate=pl.CostEstimate(flops=20_000_000_000, bytes_accessed=35_000_000, transcendentals=0),
        name="attend_back",
    )(packed, soft, att, gbr, tiles, out_w, table, hot)


def end(images, gbr, gpacked, weight, vectors):
    return pl.pallas_call(
        end_kernel,
        out_shape=(shaped((GH, GW, D), bf16), shaped((8, D), f32)),
        in_specs=[VMEM] * 5,
        out_specs=(VMEM, VMEM),
        scratch_shapes=[pltpu.VMEM((WINDOWS * WIN, LINE, D), f32)],
        compiler_params=params(),
        cost_estimate=pl.CostEstimate(flops=5_000_000_000, bytes_accessed=17_000_000, transcendentals=0),
        name="end",
    )(images, gbr, gpacked, weight, vectors)


def one_hot_keys(flip):
    token = np.arange(TOK)
    row, col = token // LINE, token % LINE
    lane = np.arange(128)
    group, local = lane // 32, lane % 32
    hot = []
    for head in range(2):
        mine = (group % 2 == head)[None, :]
        value = ((local[None, :] == row[:, None]) & (local < WIN)[None, :]) | (
            (local[None, :] - 16 == (13 - col if flip else col)[:, None]) & (col < WIN)[:, None]
        )
        value = np.where(mine & value, 1.0, 0.0)
        value[:, 14] = np.where(col >= WIN, -1e30, 0.0)
        hot.append(value)
    return jnp.asarray(np.stack(hot), dtype=bf16)


def pair_table(row_table, col_table, offset):
    rows = jnp.pad(row_table.T, ((0, 0), (0, 5)))
    cols = jnp.pad(col_table.T, ((0, 0), (0, 5)))
    zero = jnp.zeros_like(rows)

    def lanes(part):
        top = jnp.concatenate([part, zero, part, zero], axis=1)
        bottom = jnp.concatenate([zero, part, zero, part], axis=1)
        return jnp.concatenate([top, bottom], axis=0)

    return jnp.concatenate([lanes(rows), jnp.roll(lanes(cols), offset, axis=1)], axis=1)


def table_grads(total):
    rows = total[:128]
    cols = jnp.roll(total[128:], -16, axis=0)

    def pick(part):
        part = part.reshape(4, 32, 2, HD)
        value = part[0, :, 0] + part[1, :, 1] + part[2, :, 0] + part[3, :, 1]
        return value[:27]

    return pick(rows)[::-1], pick(cols)


def compute(gathered, images, grad_out, box_rows, box_cols, box_valid, box_count, row_table, col_table):
    (in_w, out_w, up_w, down_w, small) = gathered
    (qb, vb, ob, g1, s1, g2, s2, ub, db) = small
    image = images[0]
    vectors = jnp.stack([g1, s1, g2, s2, db, ob, qb, vb]).astype(f32)
    zero = jnp.zeros((1, D), f32)
    bias = jnp.concatenate([vectors[6:7], zero, vectors[7:8]], axis=1)
    table = pair_table(row_table[::-1], col_table[::-1], 3)
    table_back = pair_table(row_table[::-1], col_table, 16)
    hot = one_hot_keys(False)
    hot_back = one_hot_keys(True)
    tiles = begin(image, vectors).reshape(WINDOWS * TOK, D)
    cot, gupd = weigh(box_count, grad_out[0], box_rows[0], box_cols[0], box_valid.reshape(NBOX, 1))
    packed, soft, att, branch = forward(tiles, in_w, bias, out_w, vectors[5:6], table, hot)
    block_out, gbr, gup, gdown, gupb, sums2 = middle(
        image, branch.reshape(WINDOWS * WIN, LINE, D), cot, gupd, vectors, up_w, ub.astype(f32)[None], down_w
    )
    gpacked, gin, gout, gbias, gtab = backward(
        packed, soft, att, gbr.reshape(WINDOWS * TOK, D), tiles, out_w, table_back, hot_back
    )
    image_grad, sums1 = end(image, gbr, gpacked, in_w, vectors)
    row_grad, col_grad = table_grads(gtab)
    return (
        block_out[None],
        image_grad[None],
        gin,
        gout,
        gup,
        gdown,
        (gbias[0], gbias[1], sums2[2], sums1[0], sums1[1], sums2[0], sums2[1], gupb[0], sums2[3]),
        row_grad,
        col_grad,
    )


AXES = ("dp", "fsdp")


def gather(x):
    return lax.all_gather(x, AXES, axis=0, tiled=True)


def scatter(x):
    return lax.psum_scatter(x, AXES, scatter_dimension=0, tiled=True)


def local(
    images,
    grad_out,
    box_rows,
    box_cols,
    box_valid,
    box_count,
    in_weight,
    query_bias,
    value_bias,
    out_weight,
    out_bias,
    first_gain,
    first_shift,
    second_gain,
    second_shift,
    up_weight,
    up_bias,
    down_weight,
    down_bias,
    row_table,
    col_table,
):
    own = in_weight.shape[0]
    vectors = [query_bias, value_bias, out_bias, first_gain, first_shift, second_gain, second_shift, down_bias]
    columns = jnp.concatenate([jnp.stack(vectors, axis=1), up_bias.reshape(own, 4)], axis=1)
    columns = jnp.pad(columns, ((0, 0), (0, 128 - 12)))
    first = gather(jnp.concatenate([columns, in_weight, out_weight], axis=1))
    up_w = gather(up_weight)
    down_w = gather(down_weight)
    small = first[:, :12]
    flat = small[:, :8].T
    small = (flat[0], flat[1], flat[2], flat[3], flat[4], flat[5], flat[6], small[:, 8:].reshape(FF), flat[7])
    in_w = first[:, 128 : 128 + 3 * D]
    out_w = first[:, 128 + 3 * D :]
    block_out, image_grad, gin, gout, gup, gdown, grads, row_grad, col_grad = compute(
        (in_w, out_w, up_w, down_w, small), images, grad_out, box_rows, box_cols, box_valid, box_count, row_table, col_table
    )
    gup = scatter(gup).astype(f32)
    gdown = scatter(gdown).astype(f32)
    attention = scatter(jnp.concatenate([gin, gout], axis=1)).astype(f32)
    flat = jnp.concatenate([g for g in grads] + [row_grad.reshape(-1), col_grad.reshape(-1)])
    flat = lax.psum(flat, AXES)
    index = lax.axis_index(AXES)
    out = []
    at = 0
    for g in grads:
        size = g.shape[0]
        part = size // (D // own)
        out.append(lax.dynamic_slice(flat, (at + index * part,), (part,)))
        at += size
    table = 27 * HD
    row_grad = flat[at : at + table].reshape(27, HD)
    col_grad = flat[at + table : at + 2 * table].reshape(27, HD)
    return (
        block_out,
        image_grad,
        attention[:, : 3 * D],
        out[0],
        out[1],
        attention[:, 3 * D :],
        out[2],
        out[3],
        out[4],
        out[5],
        out[6],
        gup,
        out[7],
        gdown,
        out[8],
        row_grad,
        col_grad,
    )


def solution(mesh):
    rows = P(AXES)
    return jax.shard_map(
        local,
        mesh=mesh,
        in_specs=(rows,) * 19 + (P(), P()),
        out_specs=(rows,) * 15 + (P(), P()),
        check_vma=False,
    )
```

time: 1620 us -> 662 us (0.41)
  local copies, waits for them, and re-layouts: 515 us -> 31 us
  matrix products: 357 us -> 0 us
  other arithmetic: 259 us -> 14 us
  Pallas kernels: 0 us -> 155 us
  waiting for transfers between devices: 360 us -> 405 us
  blocking collectives: 85 us -> 40.3 us
    dot_general x54 -> x0, matrix products: 357 us -> none  [the longest x1 37.3 us: local(): jnp.einsum('rd,fd->rf', grad_update, weights_back[11], preferred_element_...]
    pallas_call x0 -> x6, Pallas kernels: none -> 155 us  [the longest x1 60.8 us: middle(): pl.pallas_call(middle_kernel, grid=(FF // CHUNK,), out_shape=(shaped((GH,...]
    all_gather x4 -> x3, waiting for transfers between devices: 0.06 us -> 138 us  [gather(): return lax.all_gather(x, AXES, axis=0, tiled=True)]
    reduce_sum x12 -> x0, other arithmetic: 112 us -> none  [the longest x2 29.9 us: normalize(): jnp.mean(center * center, axis=-1, keepdims=True) + epsilon]
    dot_general x12 -> x0, local copies, waits for them, and re-layouts: 111 us -> none  [the longest x4 46 us: score_block(): jnp.einsum('wqhc,qkc->whqk', queries, cols_low, preferred_element_type=jn...]
    convert_element_type x20 -> x4, other arithmetic: 100 us -> 4.95 us  [the longest x1 1.64 us: local(): gup = scatter(gup).astype(f32)]
    reduce_scatter x4 -> x3, waiting for transfers between devices: 357 us -> 265 us  [scatter(): return lax.psum_scatter(x, AXES, scatter_dimension=0, tiled=True)]
    while x118 -> x0, local copies, waits for them, and re-layouts: 85.1 us -> none
  transfers between devices with their start and end apart: 8 -> 6, of which waited for: 3 -> 6; matrix products, arithmetic and copies ran while one was open for 31% -> 5% of each run, Pallas kernels for 0% -> 8%
where the time goes in v1:
time: 662 us; the launch traced here: 661 us
  waiting for transfers between devices  405 us (61%)
  Pallas kernels  155 us (23%)
  blocking collectives  40.3 us (6%)
  local copies, waits for them, and re-layouts  31 us (5%)
  between operations  15 us (2%)
  other arithmetic  14 us (2%)
    reduce_scatter x3, waiting for transfers between devices, scatter(): return lax.psum_scatter(x, AXES, scatter_dimension=0, tiled=True)  265 us
    all_gather x3, waiting for transfers between devices, gather(): return lax.all_gather(x, AXES, axis=0, tiled=True)  138 us
    pallas_call x1, Pallas kernels, middle(): pl.pallas_call(middle_kernel, grid=(FF // CHUNK,), out_shape=(shaped((GH,...  60.8 us
    pallas_call x1, Pallas kernels, backward(): pl.pallas_call(backward_kernel, grid=(WINDOWS,), out_shape=(shaped((WINDO...  42.4 us
    psum x1, blocking collectives, local(): flat = lax.psum(flat, AXES)  40.3 us
    pallas_call x1, Pallas kernels, forward(): pl.pallas_call(forward_kernel, grid=(WINDOWS,), out_shape=(shaped((WINDOW...  28.9 us
    pallas_call x1, Pallas kernels, end(): pl.pallas_call(end_kernel, out_shape=(shaped((GH, GW, D), bf16), shaped((...  13.7 us
  transfers between devices with their start and end apart: 6, of which 6 were waited for; matrix products, arithmetic and copies ran while one was open for 5% of the time, Pallas kernels for 8%

profile of v1, /device:TPU:0, one launch (start us, length us, event | category | flops | bytes accessed | tf_op | source)
XLA Modules:
  0.0 661.0 jit_solution(6412429452052358385)
XLA Ops:
  7.2 0.7 copy.66
  8.0 0.7 copy.67
  8.7 0.7 copy.68
  9.5 0.7 copy.69
  10.2 0.7 copy.70
  11.0 0.7 copy.71
  11.7 0.7 copy.72
  12.5 0.7 copy.73
  13.2 0.7 reshape.105
  14.0 0.1 concatenate.61
  14.1 1.6 fusion.2
  15.8 0.7 all-gather.6.cloned.1.call-update
  16.5 0.7 all-gather.8.cloned.1.call-update
  17.2 0.8 copy.76
  18.0 0.1 rev.11
  18.2 0.1 fusion.6
  18.3 0.1 slice.205
  18.4 0.8 copy.75
  19.2 0.1 rev.10
  19.3 1.5 copy.77
  20.8 1.5 copy.78
  22.2 1.5 copy.79.valid_ref
  24.4 0.1 slice.208
  24.5 4.8 weigh.1
  29.3 0.8 pad_maximum_fusion.1.table_ref
  30.0 0.8 pad_maximum_fusion.2.table_ref
  30.8 52.1 %all-gather.4.cloned.1.call-done = bf16[768,3200]{1,0:T(8,128)(2,1)} async-done(((bf16[24,3200]{1,0:T(8,128)(2,1)}), bf16[768,3200]{1,0:T(8,128)(2,1)}) %all-gather.4.cloned.1.call-update) | async-done | bytes 4915216 | tf_op jit(solution)/shard_map/all_gather | solution.py:615
  82.9 0.9 slice.196
  83.9 0.1 copy.82
  84.0 1.0 slice_convert_fusion
  85.1 0.9 reshape.116.upb_ref
  85.9 4.0 slice.200.weight_ref
  89.9 2.4 slice.203.out_w_ref
  92.3 0.6 maximum_convert_fusion.vec_ref
  92.9 4.5 begin.1
  97.4 1.4 fusion.15
  98.8 0.6 fusion.10.bias_ref
  99.5 28.9 %attend.1 = (bf16[1344,2304]{1,0:T(8,128)(2,1)}, bf16[72,224,224]{2,1,0:T(8,128)(2,1)}, bf16[1344,768]{1,0:T(8,128)(2,1)}, f32[1344,768]{1,0:T(8,128)}) custom-call(bf16[1344,768]{1,0:T(8,128)(2,1)} %bitcast.28, bf16[768,2304]{1,0:T(8,128)(2,1)} %slice.200.weight_ref, f32[1,2304]{1,0:T(1,128)} %fusion.10.bias_ref, bf16[768,768]{1,0:T(8,128)(2,1)} %slice.203.out_w_ref, ...), custom_call_target="tpu_custom_call" | custom-call | flops 8999999488 | bytes 25000000 | tf_op jit(solution)/shard_map/attend/pallas_call | solution.py:417
  128.4 20.1 %all-gather.6.cloned.1.call-done.up_ref = bf16[768,3072]{1,0:T(8,128)(2,1)} async-done(((bf16[24,3072]{1,0:T(8,128)(2,1)}), bf16[768,3072]{1,0:T(8,128)(2,1)}) %all-gather.6.cloned.1.call-update) | async-done | bytes 4718608 | tf_op jit(solution)/shard_map/all_gather | solution.py:615
  148.5 65.5 %all-gather.8.cloned.1.call-done.down_ref = bf16[3072,768]{1,0:T(8,128)(2,1)} async-done(((bf16[96,768]{1,0:T(8,128)(2,1)}), bf16[3072,768]{1,0:T(8,128)(2,1)}) %all-gather.8.cloned.1.call-update) | async-done | bytes 4718608 | tf_op jit(solution)/shard_map/all_gather | solution.py:615
  214.0 60.8 %feed.1 = (bf16[26,38,768]{2,1,0:T(8,128)(2,1)}, bf16[84,16,768]{2,1,0:T(8,128)(2,1)}, bf16[768,3072]{1,0:T(8,128)(2,1)}, bf16[3072,768]{1,0:T(8,128)(2,1)}, f32[1,3072]{1,0:T(1,128)}, /*index=5*/f32[8,768]{1,0:T(8,128)}) custom-call(bf16[26,38,768]{2,1,0:T(8,128)(2,1)} %bitcast.31, f32[84,16,768]{2,1,0:T(8,128)} %bitcast.55, ...), custom_call_target="tpu_custom_call" | custom-call | flops 28000000000 | bytes 36000000 | tf_op jit(solution)/shard_map/feed/pallas_call | solution.py:443
  274.8 42.4 %attend_back.1 = (bf16[1344,2304]{1,0:T(8,128)(2,1)}, bf16[768,2304]{1,0:T(8,128)(2,1)}, bf16[768,768]{1,0:T(8,128)(2,1)}, f32[8,768]{1,0:T(8,128)}, f32[256,128]{1,0:T(8,128)}) custom-call(bf16[1344,2304]{1,0:T(8,128)(2,1)} %get-tuple-element.41.packed_ref, bf16[72,224,224]{2,1,0:T(8,128)(2,1)} %get-tuple-element.42.soft_ref, ...), custom_call_target="tpu_custom_call" | custom-call | flops 20000000000 | bytes 35000000 | tf_op jit(solution)/shard_map/attend_back/pallas_call | solution.py:488
  317.1 5.1 pad_maximum_fusion
  322.3 0.5 reduce-scatter.6.cloned.1.call-update
  322.8 0.3 reduce-scatter.8.cloned.1.call-start
  323.1 0.3 reduce-scatter.8.cloned.1.call-update
  323.5 0.1 reshape.112
  323.8 0.1 reshape.110
  324.1 13.7 %end.1 = (bf16[26,38,768]{2,1,0:T(8,128)(2,1)}, f32[8,768]{1,0:T(8,128)}) custom-call(bf16[26,38,768]{2,1,0:T(8,128)(2,1)} %bitcast.32, bf16[84,16,768]{2,1,0:T(8,128)(2,1)} %get-tuple-element.40.gbr_ref, bf16[1344,2304]{1,0:T(8,128)(2,1)} %get-tuple-element.44.gpacked_ref, bf16[768,2304]{1,0:T(8,128)(2,1)} %slice.200.weight_ref, ...), custom_call_target="tpu_custom_call" | custom-call | flops 5000000000 | bytes 17000000 | tf_op jit(solution)/shard_map/end/pallas_call | solution.py:522
  337.9 0.8 slice_reduce_fusion.3
  338.7 0.8 slice_reduce_fusion.6
  339.6 0.1 concatenate.77
  339.7 40.3 %psum.7 = f32[12672]{0:T(1024)S(1)} all-reduce(f32[12672]{0:T(1024)S(1)} %concatenate.77), channel_id=1, replica_groups=mesh['dp'=4,'fsdp'=8] {'dp','fsdp'}, use_global_device_ids=true, to_apply=%region_1.2 | all-reduce | flops 12672 | bytes 101376 | tf_op jit(solution)/shard_map/psum | solution.py:664
  380.1 0.7 reshape.114
  380.8 0.7 reshape.115
  381.4 0.6 dynamic_slice.34
  382.0 0.6 fusion.14
  382.6 46.1 %reduce-scatter.4.cloned.1.call-done = bf16[24,3072]{1,0:T(8,128)(2,1)} async-done(((bf16[768,3072]{1,0:T(8,128)(2,1)}), bf16[24,3072]{1,0:T(8,128)(2,1)}) %reduce-scatter.4.cloned.1.call-update) | async-done | bytes 147472 | tf_op jit(solution)/shard_map/reduce_scatter | solution.py:619
  428.8 1.6 slice.210
  430.4 1.4 slice.227
  431.8 109.3 %reduce-scatter.6.cloned.1.call-done = bf16[24,3072]{1,0:T(8,128)(2,1)} async-done(((bf16[768,3072]{1,0:T(8,128)(2,1)}), bf16[24,3072]{1,0:T(8,128)(2,1)}) %reduce-scatter.6.cloned.1.call-update) | async-done | bytes 147472 | tf_op jit(solution)/shard_map/reduce_scatter | solution.py:619
  541.1 1.6 convert_element_type.36
  542.7 109.8 %reduce-scatter.8.cloned.1.call-done = bf16[96,768]{1,0:T(8,128)(2,1)} async-done(((bf16[3072,768]{1,0:T(8,128)(2,1)}), bf16[96,768]{1,0:T(8,128)(2,1)}) %reduce-scatter.8.cloned.1.call-update) | async-done | bytes 147472 | tf_op jit(solution)/shard_map/reduce_scatter | solution.py:619
  652.5 1.6 convert_element_type.37
  (36 shorter events, 0.8 us)
Async XLA Ops:
  7.2 75.7 %all-gather.4.cloned.1.call-start = ((), (), s32[]{:S(2)}) async-start(), calls=%async_computation.3 | async-start | bytes 5068800 | tf_op jit(solution)/shard_map/all_gather | solution.py:615
  15.7 132.7 %all-gather.6.cloned.1.call-start = ((), (), s32[]{:S(2)}) async-start(), calls=%async_computation.4 | async-start | bytes 4866048 | tf_op jit(solution)/shard_map/all_gather | solution.py:615
  16.5 197.5 %all-gather.8.cloned.1.call-start = ((), (), s32[]{:S(2)}) async-start(), calls=%async_computation.5 | async-start | bytes 4866048 | tf_op jit(solution)/shard_map/all_gather | solution.py:615
  17.2 411.6 %reduce-scatter.4.cloned.1.call-start = ((), (), s32[]{:S(2)}) async-start(), calls=%async_computation.6 | async-start | bytes 4866048 | tf_op jit(solution)/shard_map/reduce_scatter | solution.py:619
  322.2 218.9 %reduce-scatter.6.cloned.1.call-start = ((), (), s32[]{:S(2)}) async-start(), calls=%async_computation.7 | async-start | bytes 4866048 | tf_op jit(solution)/shard_map/reduce_scatter | solution.py:619
  322.3 1.1 copy-start
  322.8 329.7 %reduce-scatter.8.cloned.1.call-start = ((), (), s32[]{:S(2)}) async-start(), calls=%async_computation.8 | async-start | bytes 4866048 | tf_op jit(solution)/shard_map/reduce_scatter | solution.py:619
  324.1 15.4 %copy-start.2 = (f32[8,768]{1,0:T(8,128)S(1)}, f32[8,768]{1,0:T(8,128)}, u32[]{:S(2)}) copy-start(f32[8,768]{1,0:T(8,128)} %get-tuple-element.49) | copy-start | bytes 73732
  324.1 15.5 %copy-start.1 = (f32[1,3072]{1,0:T(1,128)S(1)}, f32[1,3072]{1,0:T(1,128)}, u32[]{:S(2)}) copy-start(f32[1,3072]{1,0:T(1,128)} %get-tuple-element.51) | copy-start | bytes 36868
Sparse Core Ops, SparseCore 0:
  15.8 67.0 all-gather.3
  85.9 62.4 all-gather.5
  151.4 62.4 all-gather.7
  322.3 106.3 reduce-scatter.3
  435.0 106.0 reduce-scatter.5
  546.4 106.0 reduce-scatter.7

commit v2 on v1

v2 whole, which is shorter than its diff:
```python
import functools

import jax
import jax.numpy as jnp
import numpy as np
from jax import lax
from jax.experimental import pallas as pl
from jax.experimental.pallas import tpu as pltpu
from jax.sharding import PartitionSpec as P

D = 768
HEADS = 12
HD = 64
FF = 3072
WIN = 14
GH = 26
GW = 38
NBOX = 300
ACROSS = 3
WINDOWS = 6
LINE = 16
TOK = WIN * LINE
REAL = GH * GW
DENSE = 992
PAIRS = HEADS // 2
STARTS = (0, 14, 28)
WIDTHS = (14, 14, 10)
CHUNK = 768
CALLS = 3
SPLITS = ((0, 256), (256, 256), (512, 256), (768, 224))
epsilon = 1e-06
f32 = jnp.float32
bf16 = jnp.bfloat16
LIMIT = 60 * 1024 * 1024


def dot(a, b):
    return lax.dot_general(a, b, (((1,), (0,)), ((), ())), preferred_element_type=f32)


def dot_bt(a, b):
    return lax.dot_general(a, b, (((1,), (1,)), ((), ())), preferred_element_type=f32)


def dot_at(a, b):
    return lax.dot_general(a, b, (((0,), (0,)), ((), ())), preferred_element_type=f32)


def unit_of(x):
    center = x - jnp.mean(x, axis=-1, keepdims=True)
    inverse = lax.rsqrt(jnp.mean(center * center, axis=-1, keepdims=True) + epsilon)
    return center * inverse, inverse


def norm_back(grad, unit, inverse, gain):
    scaled = grad * gain
    return inverse * (
        scaled
        - jnp.mean(scaled, axis=-1, keepdims=True)
        - unit * jnp.mean(scaled * unit, axis=-1, keepdims=True)
    )


def place_of(row):
    return (row // WIN) * ACROSS, row % WIN


def spread_row(row, value, out_ref):
    first, place = place_of(row)
    for piece, (start, width) in enumerate(zip(STARTS, WIDTHS)):
        part = value[start : start + width]
        part = jnp.concatenate([part, jnp.zeros((LINE - width, part.shape[1]), part.dtype)], axis=0)
        out_ref[(first + piece) * WIN + place] = part.astype(out_ref.dtype)


def join_row(row, refs):
    first, place = place_of(row)
    each = WINDOWS // len(refs)
    parts = []
    for piece, width in enumerate(WIDTHS):
        window = first + piece
        line = refs[window // each][(window % each) * WIN + place]
        parts.append(line.astype(f32)[:width])
    return jnp.concatenate(parts, axis=0)


def begin_kernel(img_ref, *refs):
    unit_ref, flag_ref = refs[-2:]
    flag_ref[0] = 0
    unit_ref[...] = jnp.zeros_like(unit_ref)
    for row in range(GH):
        unit, _ = unit_of(img_ref[row].astype(f32))
        spread_row(row, unit, unit_ref)


def pair_tables(row_table, col_table, entry_row, entry_col):
    parts = []
    for table, place in ((row_table, entry_row), (col_table, entry_col)):
        pieces = jnp.zeros((128, 128), f32)
        entries = lax.broadcasted_iota(jnp.int32, (2 * WIN - 1, 128), 0)
        lane = lane_iota((2 * WIN - 1, 128))
        row = lax.broadcasted_iota(jnp.int32, (128, 128), 0)
        for head in range(2):
            where = place(entries) + 32 * head
            pick = ((lane - where) % 64) == 0
            spread = dot_at(table, jnp.where(pick, 1.0, 0.0).astype(bf16))
            both = jnp.concatenate([spread, spread], axis=0)
            pieces = jnp.where((row < HD) == (head == 0), both, pieces)
        parts.append(pieces)
    return jnp.concatenate(parts, axis=1).astype(bf16)


def weight_kernel(count_ref, grad_ref, rows_ref, cols_ref, valid_ref, rowt_ref, colt_ref, *refs):
    cot_ref, upd_ref, table_ref, back_ref, flag_ref = refs[-5:]
    flag_ref[0] = 0
    table_ref[...] = pair_tables(rowt_ref[...], colt_ref[...], lambda e: 26 - e, lambda e: 29 - e)
    back_ref[...] = pair_tables(rowt_ref[...], colt_ref[...], lambda e: 26 - e, lambda e: 16 + e)
    slot = lax.broadcasted_iota(jnp.int32, (NBOX, 1), 0)
    live = (slot < count_ref[0]) & (valid_ref[...] == 1)
    rows = rows_ref[...]
    cols = cols_ref[...]
    top = jnp.minimum(rows[:, 0:1], rows[:, 1:2])
    low = jnp.maximum(rows[:, 0:1], rows[:, 1:2])
    left = jnp.minimum(cols[:, 0:1], cols[:, 1:2])
    right = jnp.maximum(cols[:, 0:1], cols[:, 1:2])
    grid_r = lax.broadcasted_iota(jnp.int32, (NBOX, GH), 1)
    grid_c = lax.broadcasted_iota(jnp.int32, (NBOX, GW), 1)
    in_rows = jnp.where((grid_r >= top) & (grid_r < low) & live, 1.0, 0.0)
    in_cols = jnp.where((grid_c >= left) & (grid_c < right), 1.0, 0.0)
    inside = dot_at(in_cols.astype(bf16), in_rows.astype(bf16))
    total = jnp.sum(jnp.where(live, 1.0, 0.0))
    weight = 1.0 + 2.0 * inside / jnp.maximum(total, 1.0)
    for row in range(GH):
        cot_ref[row * GW : (row + 1) * GW, :] = grad_ref[row].astype(f32) * weight[:, row : row + 1]
    cot_ref[REAL:, :] = jnp.zeros((DENSE - REAL, D), f32)
    upd_ref[...] = cot_ref[...].astype(bf16)


def lane_iota(shape):
    return lax.broadcasted_iota(jnp.int32, shape, len(shape) - 1)


def position_terms(queries, table):
    both = dot(queries, table)
    row_part = both[:, :128].reshape(WIN, LINE, 128)
    col_part = both[:, 128:].reshape(WIN, LINE, 128)
    lane = lane_iota((LINE, 128))
    local = lane % 32
    out = []
    for place in range(WIN):
        rolled_r = pltpu.roll(row_part[place], (place - 13) % 128, 1)
        rolled_c = pltpu.roll(col_part[place], 0, 1, stride=1, stride_axis=0)
        value = jnp.where(local < 16, rolled_r, rolled_c)
        high = value.astype(bf16).astype(f32)
        value = jnp.where(lane < 64, high, value - high)
        value = jnp.where(lane == 14, 1.0, value)
        out.append(value)
    return jnp.concatenate(out, axis=0).astype(bf16)


def keep_head(value, head):
    lane = lane_iota(value.shape)
    return jnp.where((lane < HD) == (head == 0), value, jnp.zeros_like(value))


def forward_kernel(call, unit_ref, one_ref, two_ref, table_ref, hot_ref, *refs):
    if call == 0:
        core_ref, one_half, two_half = unit_ref, one_ref, two_ref
        one_other, two_other, unit_ref, table_ref, hot_ref = table_ref, hot_ref, *refs[:3]
        refs, (one_ref, two_ref, sems) = refs[:-3], refs[-3:]
    tiles_ref, packed_ref, soft_ref, att_ref, branch_ref, vec_ref, flag_ref = refs[-7:]
    step = pl.program_id(0)

    @pl.when(step == 0)
    def _():
        if call == 0:
            core = core_ref[1]
            made = []
            for i, (half, whole_ref, place) in enumerate(
                [
                    (one_half, one_ref, core),
                    (two_half, two_ref, core),
                    (one_other, one_ref, 1 - core),
                    (two_other, two_ref, 1 - core),
                ]
            ):
                for y in range(2):
                    here = pl.ds(pl.multiple_of((2 * y + place) * (D // 4), D // 4), D // 4)
                    copy = pltpu.make_async_copy(half.at[y], whole_ref.at[here, :], sems.at[2 * i + y])
                    copy.start()
                    made.append(copy)
            for copy in made:
                copy.wait()
        vec_ref[...] = one_ref[:, :128].astype(f32).T[:16]
        flag_ref[0] = 0

    window = call * (WINDOWS // CALLS) + step
    token = lax.broadcasted_iota(jnp.int32, (TOK, 1), 0)
    row_limit = jnp.where(window < ACROSS, WIN, GH - WIN)
    col_limit = jnp.where(window % ACROSS == ACROSS - 1, WIDTHS[2], WIN)
    valid = (token // LINE < row_limit) & (token % LINE < col_limit)
    tiles_ref[...] = (unit_ref[...] * vec_ref[3:4, :] + jnp.where(valid, vec_ref[4:5, :], 0.0)).astype(bf16)
    tiles = tiles_ref[...]
    packed_ref[:, :D] = (dot(tiles, one_ref[:, 128 : 128 + D]) + vec_ref[0:1, :]).astype(bf16)
    packed_ref[:, D : 2 * D] = dot(tiles, one_ref[:, 128 + D :]).astype(bf16)
    packed_ref[:, 2 * D :] = (dot(tiles, two_ref[:, :D]) + vec_ref[1:2, :]).astype(bf16)
    for pair in range(PAIRS):
        at = pair * 128
        queries = packed_ref[:, at : at + 128]
        keys = packed_ref[:, D + at : D + at + 128]
        values = packed_ref[:, 2 * D + at : 2 * D + at + 128]
        left = jnp.concatenate([queries, position_terms(queries, table_ref[...])], axis=1)
        parts = []
        for head in range(2):
            scaled = (keep_head(keys.astype(f32), head) * 0.125).astype(bf16)
            right = jnp.concatenate([scaled, hot_ref[head]], axis=1)
            scores = dot_bt(left, right)
            power = jnp.exp(scores - jnp.max(scores, axis=-1, keepdims=True))
            soft = (power * (1.0 / jnp.sum(power, axis=-1, keepdims=True))).astype(bf16)
            soft_ref[2 * pair + head] = soft
            parts.append(dot(soft, values))
        lane = lane_iota((TOK, 128))
        att_ref[:, at : at + 128] = jnp.where(lane < HD, parts[0], parts[1]).astype(bf16)
    branch_ref[...] = dot(att_ref[...], two_ref[:, D:]) + vec_ref[2:3, :]


def backward_kernel(packed_ref, soft_ref, att_ref, gbr_ref, two_ref, table_ref, hot_ref, *refs):
    gpacked_ref, gbias_ref, gtab_ref, flag_ref, gatt_ref = refs[-5:]

    @pl.when(pl.program_id(0) == 0)
    def _():
        flag_ref[0] = 0
        gbias_ref[...] = jnp.zeros_like(gbias_ref)
        gtab_ref[...] = jnp.zeros_like(gtab_ref)

    gatt_ref[...] = dot_bt(gbr_ref[...], two_ref[:, D:]).astype(bf16)
    lane = lane_iota((LINE, 128))
    local = lane % 32
    wide = lane_iota((TOK, 128))
    for pair in range(PAIRS):
        at = pair * 128
        queries = packed_ref[:, at : at + 128]
        keys = packed_ref[:, D + at : D + at + 128]
        values = packed_ref[:, 2 * D + at : 2 * D + at + 128]
        gatt = gatt_ref[:, at : at + 128]
        product = gatt.astype(f32) * att_ref[:, at : at + 128].astype(f32)
        left = []
        right = []
        gvalues = []
        gkeys = []
        for head in range(2):
            soft = soft_ref[2 * pair + head]
            delta = jnp.sum(keep_head(product, head), axis=-1, keepdims=True)
            gprobs = dot_bt(gatt, keep_head(values.astype(f32), head).astype(bf16))
            gscores = (soft.astype(f32) * (gprobs - delta)).astype(bf16)
            scaled = (keep_head(keys.astype(f32), head) * 0.125).astype(bf16)
            left.append(gscores)
            right.append(jnp.concatenate([scaled, hot_ref[head]], axis=1))
            gvalues.append(dot_at(soft, gatt))
            gkeys.append(dot_at(gscores, queries))
        both = dot(left[0], right[0]) + dot(left[1], right[1])
        terms = both[:, 128:].reshape(WIN, LINE, 128)
        rolled = []
        for place in range(WIN):
            value = terms[place]
            high = value.astype(bf16).astype(f32)
            value = jnp.where(lane < 64, high, value - high)
            row_part = jnp.where(local < WIN, value, 0.0)
            col_part = jnp.where((local >= 16) & (local < 16 + WIN), value, 0.0)
            row_part = pltpu.roll(row_part, 13 - place, 1)
            col_part = pltpu.roll(col_part, 0, 1, stride=1, stride_axis=0)
            rolled.append(jnp.concatenate([row_part, col_part], axis=1))
        rolled = jnp.concatenate(rolled, axis=0).astype(bf16)
        gqueries = both[:, :128] + dot_bt(rolled, table_ref[...])
        gtab_ref[...] += dot_at(rolled, queries)
        gq = gqueries.astype(bf16)
        gk = (jnp.where(wide < HD, gkeys[0], gkeys[1]) * 0.125).astype(bf16)
        gv = jnp.where(wide < HD, gvalues[0], gvalues[1]).astype(bf16)
        gpacked_ref[:, at : at + 128] = gq
        gpacked_ref[:, D + at : D + at + 128] = gk
        gpacked_ref[:, 2 * D + at : 2 * D + at + 128] = gv
        gbias_ref[0:1, at : at + 128] += jnp.sum(gq.astype(f32), axis=0, keepdims=True)
        gbias_ref[1:2, at : at + 128] += jnp.sum(gv.astype(f32), axis=0, keepdims=True)


def halve(core, value, keep_ref, send_ref, at):
    size = value.shape[0] // 4

    def put(first, second):
        for y in range(2):
            first[y * size : (y + 1) * size, at] = value[2 * y * size : (2 * y + 1) * size]
            second[y * size : (y + 1) * size, at] = value[(2 * y + 1) * size : (2 * y + 2) * size]

    @pl.when(core == 0)
    def _():
        put(keep_ref, send_ref)

    @pl.when(core == 1)
    def _():
        put(send_ref, keep_ref)


def attention_weights_kernel(core_ref, *refs):
    keep_ref, send_ref, flag_ref, gpacked_all, tiles_all = refs[-5:]
    flag_ref[0] = 0
    size = WINDOWS * TOK // CALLS
    for i in range(CALLS):
        gpacked_all[i * size : (i + 1) * size, :] = refs[2 * i][...]
        tiles_all[i * size : (i + 1) * size, :] = refs[2 * i + 1][...]
    for part in range(0, 3 * D, D):
        value = dot_at(tiles_all[...], gpacked_all[:, part : part + D]).astype(bf16)
        halve(core_ref[0], value, keep_ref, send_ref, slice(part, part + D))


def gelu_parts(hidden):
    size = jnp.abs(hidden)
    power = jnp.exp(hidden * hidden * -0.5)
    denominator = 1.0 + (0.3275911 * 0.7071067811865476) * size
    near = pl.reciprocal(denominator, approx=True)
    near = near * (2.0 - denominator * near)
    series = near * (
        0.254829592
        + near * (-0.284496736 + near * (1.421413741 + near * (-1.453152027 + near * 1.061405429)))
    )
    tail = 0.5 * series * power
    normal = jnp.where(hidden >= 0, 1.0 - tail, tail)
    return hidden * normal, normal + hidden * power * 0.3989422804014327


def middle_kernel(
    core_ref,
    img_ref,
    cot_ref,
    gupd_ref,
    vec_ref,
    up_ref,
    down_ref,
    *refs,
):
    branch_refs = refs[:CALLS]
    att_refs = refs[CALLS : 2 * CALLS]
    out_ref, gbr_ref, gupk_ref, gups_ref, gdownk_ref, gdowns_ref, gupb_ref, sums_ref = refs[2 * CALLS : 2 * CALLS + 8]
    mid, normed, update, gnorm, active, ghidden = refs[2 * CALLS + 8 :]
    step = pl.program_id(0)
    gain = vec_ref[5:6, :]
    shift = vec_ref[6:7, :]

    @pl.when(step == 0)
    def _():
        for row in range(GH):
            mid[row * GW : (row + 1) * GW, :] = img_ref[row].astype(f32) + join_row(row, branch_refs)
        mid[REAL:, :] = jnp.zeros((DENSE - REAL, D), f32)
        update[...] = jnp.zeros_like(update)
        gnorm[...] = jnp.zeros_like(gnorm)

        def chunk(index, carry):
            here = pl.ds(pl.multiple_of(index * 32, 32), 32)
            unit, _ = unit_of(mid[here, :])
            normed[here, :] = (unit * gain + shift).astype(bf16)
            return carry

        lax.fori_loop(0, DENSE // 32, chunk, 0)

    @pl.when(step < FF // CHUNK)
    def _():
        up_bias = vec_ref[pl.ds(8 + step, 1), :]
        for start, size in SPLITS:
            here = slice(start, start + size)
            hidden = dot(normed[here, :], up_ref[...]) + up_bias
            gactive = dot_bt(gupd_ref[here, :], down_ref[...])
            act, slope = gelu_parts(hidden)
            act = act.astype(bf16)
            gh = (gactive * slope).astype(bf16)
            active[here, :] = act
            ghidden[here, :] = gh
            update[here, :] += dot(act, down_ref[...])
            gnorm[here, :] += dot_bt(gh, up_ref[...])
        gupb_ref[pl.ds(step, 1), :] = jnp.sum(ghidden[...].astype(f32), axis=0, keepdims=True)
        gdown = dot_at(active[...], gupd_ref[...]).astype(bf16)
        halve(core_ref[0], gdown, gdownk_ref, gdowns_ref, slice(None))
        gup = dot_at(normed[...], ghidden[...]).astype(bf16)
        halve(core_ref[0], gup, gupk_ref, gups_ref, slice(None))

    @pl.when(step == FF // CHUNK)
    def _():
        down_bias = vec_ref[7:8, :]
        for row in range(GH):
            here = slice(row * GW, (row + 1) * GW)
            out_ref[row] = (mid[here, :] + update[here, :] + down_bias).astype(bf16)

        def chunk(index, carry):
            here = pl.ds(pl.multiple_of(index * 32, 32), 32)
            unit, inverse = unit_of(mid[here, :])
            grad = gnorm[here, :]
            cot = cot_ref[here, :]
            result = cot + norm_back(grad, unit, inverse, gain)
            rounded = result.astype(bf16).astype(f32)
            update[here, :] = rounded
            gain_sum, shift_sum, branch_sum, bias_sum = carry
            return (
                gain_sum + jnp.sum((grad * unit).reshape(4, 8, D), axis=0),
                shift_sum + jnp.sum(grad.reshape(4, 8, D), axis=0),
                branch_sum + jnp.sum(rounded.reshape(4, 8, D), axis=0),
                bias_sum + jnp.sum(cot.astype(bf16).astype(f32).reshape(4, 8, D), axis=0),
            )

        zero = jnp.zeros((8, D), f32)
        sums = lax.fori_loop(0, DENSE // 32, chunk, (zero,) * 4)
        sums_ref[...] = jnp.concatenate(
            [jnp.sum(s, axis=0, keepdims=True) for s in sums] + [jnp.zeros((4, D), f32)], axis=0
        )
        gbr_ref[...] = jnp.zeros_like(gbr_ref)
        for row in range(GH):
            spread_row(row, update[row * GW : (row + 1) * GW, :], gbr_ref)
        each = WINDOWS * WIN // CALLS
        gout = jnp.zeros((D, D), f32)
        for i, att_ref in enumerate(att_refs):
            gout += dot_at(att_ref[...], gbr_ref[i * each : (i + 1) * each].reshape(each * LINE, D))
        halve(core_ref[0], gout.astype(bf16), gupk_ref, gups_ref, slice(None))


def end_kernel(img_ref, gbr_ref, one_ref, two_ref, vec_ref, *refs):
    gpacked_refs = refs[:CALLS]
    out_ref, sums_ref, gtiles = refs[-3:]
    gain = vec_ref[3:4, :]
    each = WINDOWS // CALLS
    for window in range(WINDOWS):
        here = slice((window % each) * TOK, (window % each + 1) * TOK)
        gpacked_ref = gpacked_refs[window // each]
        value = dot_bt(gpacked_ref[here, : 2 * D], one_ref[:, 128:]) + dot_bt(gpacked_ref[here, 2 * D :], two_ref[:, :D])
        gtiles[window * WIN : (window + 1) * WIN] = value.reshape(WIN, LINE, D)
    gain_sum = jnp.zeros((1, D), f32)
    shift_sum = jnp.zeros((1, D), f32)
    for row in range(GH):
        unit, inverse = unit_of(img_ref[row].astype(f32))
        grad = join_row(row, [gtiles])
        gain_sum += jnp.sum(grad * unit, axis=0, keepdims=True)
        shift_sum += jnp.sum(grad, axis=0, keepdims=True)
        out_ref[row] = (join_row(row, [gbr_ref]) + norm_back(grad, unit, inverse, gain)).astype(bf16)
    sums_ref[...] = jnp.concatenate([gain_sum, shift_sum, jnp.zeros((6, D), f32)], axis=0)


def pack_kernel(eight_ref, upb_ref, weight_ref, out_ref):
    own = weight_ref.shape[0]
    flat = upb_ref[...].astype(f32)
    rows = [eight_ref[...].astype(f32)] + [flat[:, own * i : own * (i + 1)] for i in range(4)]
    rows = jnp.concatenate(rows, axis=0)
    rows = jnp.concatenate([rows, jnp.zeros((12, 128 - own), f32)], axis=1)
    square = jnp.concatenate([rows, jnp.zeros((116, 128), f32)], axis=0)
    out_ref[:, :128] = square.T[:own].astype(bf16)
    out_ref[:, 128:] = weight_ref[:, : 2 * D]


def regroup(value, own, back=False):
    count = value.shape[1] // (4 * own)
    parts = []
    for i in range(count if back else 4):
        for j in range(4 if back else count):
            at = (j * count + i) * own if back else (4 * j + i) * own
            parts.append(value[:, at : at + own])
    return jnp.concatenate(parts, axis=1)


def pack_feed_kernel(up_ref, down_ref, out_ref):
    own = up_ref.shape[0]
    out_ref[:, :FF] = regroup(up_ref[...].astype(f32), own).astype(bf16)
    for k in range(4):
        part = down_ref[...].astype(f32)[k * own : (k + 1) * own]
        out_ref[:, FF + k * D : FF + (k + 1) * D] = part.astype(bf16)


def unpack_feed_kernel(first_ref, first_recv_ref, second_ref, second_recv_ref, up_ref, out_ref, down_ref):
    own = up_ref.shape[0]
    first = first_ref[...] + first_recv_ref[...].astype(f32)
    up_ref[...] = regroup(first[:, :FF], own, back=True)
    out_ref[...] = first[:, FF:]
    second = second_ref[...] + second_recv_ref[...].astype(f32)
    for k in range(4):
        down_ref[k * own : (k + 1) * own, :] = second[:, k * D : (k + 1) * D]


def params(steps=0):
    return pltpu.CompilerParams(
        vmem_limit_bytes=LIMIT, dimension_semantics=("arbitrary",) * steps if steps else None
    )


VMEM = pl.BlockSpec(memory_space=pltpu.VMEM)
SMEM = pl.BlockSpec(memory_space=pltpu.SMEM)


def whole(shape):
    return pl.BlockSpec(shape, lambda i: (0,) * len(shape))


def shaped(shape, dtype):
    return jax.ShapeDtypeStruct(shape, dtype)


def pack_feed(up, down):
    own = up.shape[0]
    return pl.pallas_call(
        pack_feed_kernel,
        out_shape=shaped((own, 2 * FF), bf16),
        in_specs=[VMEM] * 2,
        out_specs=VMEM,
        compiler_params=params(),
        name="pack_feed",
    )(up, down)


def unpack_feed(first, second):
    flat = [value.reshape(value.shape[-2:]) for value in first + second]
    own = flat[0].shape[0]
    return pl.pallas_call(
        unpack_feed_kernel,
        out_shape=(shaped((own, FF), f32), shaped((own, D), f32), shaped((4 * own, D), f32)),
        in_specs=[VMEM] * 4,
        out_specs=(VMEM,) * 3,
        compiler_params=params(),
        name="unpack_feed",
    )(*flat)


FLAG = pl.BlockSpec(memory_space=pltpu.SMEM)
ANY = pl.BlockSpec(memory_space=pl.ANY)
flag_shape = jax.ShapeDtypeStruct((1,), jnp.int32)


def begin(images, before):
    return pl.pallas_call(
        begin_kernel,
        out_shape=(shaped((WINDOWS * WIN, LINE, D), f32), flag_shape),
        in_specs=[VMEM] + [ANY] * len(before),
        out_specs=(VMEM, FLAG),
        compiler_params=params(),
        cost_estimate=pl.CostEstimate(flops=30_000_000, bytes_accessed=6_000_000, transcendentals=0),
        name="begin",
    )(images, *before)


def weigh(count, grad_out, rows, cols, valid, row_table, col_table, before):
    return pl.pallas_call(
        weight_kernel,
        out_shape=(
            shaped((DENSE, D), f32),
            shaped((DENSE, D), bf16),
            shaped((128, 256), bf16),
            shaped((128, 256), bf16),
            flag_shape,
        ),
        in_specs=[SMEM] + [VMEM] * 6 + [ANY] * len(before),
        out_specs=(VMEM,) * 4 + (FLAG,),
        compiler_params=params(),
        cost_estimate=pl.CostEstimate(flops=30_000_000, bytes_accessed=6_000_000, transcendentals=0),
        name="weigh",
    )(count, grad_out, rows, cols, valid, row_table, col_table, *before)


def forward(call, unit, weights, table, hot, before=()):
    per = lambda *shape: pl.BlockSpec(shape, lambda i: (i,) + (0,) * (len(shape) - 1))
    each = WINDOWS // CALLS
    both = [((D, 128 + 2 * D), bf16), ((D, 2 * D), bf16)]
    if call == 0:
        specs = [SMEM] + [ANY] * 4
        more_shapes = tuple(shaped(*b) for b in both)
        more_specs = tuple(whole(b[0]) for b in both)
        scratch = [pltpu.SemaphoreType.DMA((8,))]
    else:
        specs, more_shapes, more_specs, scratch = [], (), (), []
    tail = [whole(b[0]) for b in both] if call else []
    return pl.pallas_call(
        functools.partial(forward_kernel, call),
        grid=(each,),
        out_shape=(
            shaped((each * TOK, D), bf16),
            shaped((each * TOK, 3 * D), bf16),
            shaped((each * HEADS, TOK, TOK), bf16),
            shaped((each * TOK, D), bf16),
            shaped((each * TOK, D), f32),
            shaped((16, D), f32),
            flag_shape,
        )
        + more_shapes,
        in_specs=specs
        + [pl.BlockSpec((TOK, D), lambda i: (call * each + i, 0))]
        + tail
        + [whole((128, 256)), whole((2, TOK, 128))]
        + [ANY] * len(before),
        out_specs=(per(TOK, D), per(TOK, 3 * D), per(HEADS, TOK, TOK), per(TOK, D), per(TOK, D), whole((16, D)), FLAG)
        + more_specs,
        scratch_shapes=scratch,
        compiler_params=params(1),
        cost_estimate=pl.CostEstimate(flops=10_000_000_000, bytes_accessed=9_000_000, transcendentals=1_300_000),
        name="attend",
    )(*(list(weights) + [unit] if call == 0 else [unit] + list(weights)), table, hot, *before)


def middle(core, images, cot, gupd, vec, weights, branches, attended):
    steps = FF // CHUNK
    at = lambda i: jnp.minimum(i, steps - 1)
    return pl.pallas_call(
        middle_kernel,
        grid=(steps + 1,),
        out_shape=(
            shaped((GH, GW, D), bf16),
            shaped((WINDOWS * WIN, LINE, D), bf16),
            shaped((D // 2, FF + D), bf16),
            shaped((D // 2, FF + D), bf16),
            shaped((D // 2, FF), bf16),
            shaped((D // 2, FF), bf16),
            shaped((8, D), f32),
            shaped((8, D), f32),
        ),
        in_specs=[
            SMEM,
            whole((GH, GW, D)),
            whole((DENSE, D)),
            whole((DENSE, D)),
            whole((16, D)),
            pl.BlockSpec((D, CHUNK), lambda i: (0, at(i))),
            pl.BlockSpec((D, CHUNK), lambda i: (0, steps + at(i))),
        ]
        + [whole((WINDOWS // CALLS * WIN, LINE, D))] * CALLS
        + [whole((WINDOWS // CALLS * TOK, D))] * CALLS,
        out_specs=(
            whole((GH, GW, D)),
            whole((WINDOWS * WIN, LINE, D)),
            pl.BlockSpec((D // 2, CHUNK), lambda i: (0, i)),
            pl.BlockSpec((D // 2, CHUNK), lambda i: (0, i)),
            pl.BlockSpec((D // 2, CHUNK), lambda i: (0, at(i))),
            pl.BlockSpec((D // 2, CHUNK), lambda i: (0, at(i))),
            whole((8, D)),
            whole((8, D)),
        ),
        scratch_shapes=[
            pltpu.VMEM((DENSE, D), f32),
            pltpu.VMEM((DENSE, D), bf16),
            pltpu.VMEM((DENSE, D), f32),
            pltpu.VMEM((DENSE, D), f32),
            pltpu.VMEM((DENSE, CHUNK), bf16),
            pltpu.VMEM((DENSE, CHUNK), bf16),
        ],
        compiler_params=params(1),
        cost_estimate=pl.CostEstimate(flops=50_000_000_000, bytes_accessed=36_000_000, transcendentals=6_000_000),
        name="feed",
    )(core, images, cot, gupd, vec, weights, weights, *branches, *attended)


def backward(call, packed, soft, att, gbr, two, table, hot, before=()):
    per = lambda *shape: pl.BlockSpec(shape, lambda i: (i,) + (0,) * (len(shape) - 1))
    each = WINDOWS // CALLS
    return pl.pallas_call(
        backward_kernel,
        grid=(each,),
        out_shape=(
            shaped((each * TOK, 3 * D), bf16),
            shaped((8, D), f32),
            shaped((256, 128), f32),
            flag_shape,
        ),
        in_specs=[
            per(TOK, 3 * D),
            per(HEADS, TOK, TOK),
            per(TOK, D),
            pl.BlockSpec((TOK, D), lambda i: (call * each + i, 0)),
            whole((D, 2 * D)),
            whole((128, 256)),
            whole((2, TOK, 128)),
        ]
        + [ANY] * len(before),
        out_specs=(per(TOK, 3 * D), whole((8, D)), whole((256, 128)), FLAG),
        scratch_shapes=[pltpu.VMEM((TOK, D), bf16)],
        compiler_params=params(1),
        cost_estimate=pl.CostEstimate(flops=12_000_000_000, bytes_accessed=9_000_000, transcendentals=0),
        name="attend_back",
    )(packed, soft, att, gbr, two, table, hot, *before)


def attention_weights(core, parts, before=()):
    size = WINDOWS * TOK // CALLS
    operands = [array for part in parts for array in part]
    return pl.pallas_call(
        attention_weights_kernel,
        grid=(1,),
        out_shape=(shaped((D // 2, 3 * D), bf16),) * 2 + (flag_shape,),
        in_specs=[SMEM] + [whole((size, 3 * D)), whole((size, D))] * CALLS + [ANY] * len(before),
        out_specs=(whole((D // 2, 3 * D)),) * 2 + (FLAG,),
        scratch_shapes=[pltpu.VMEM((WINDOWS * TOK, 3 * D), bf16), pltpu.VMEM((WINDOWS * TOK, D), bf16)],
        compiler_params=params(1),
        cost_estimate=pl.CostEstimate(flops=25_000_000_000, bytes_accessed=18_000_000, transcendentals=0),
        name="attend_weights",
    )(core, *operands, *before)


def end(images, gbr, one, two, vec, gpacked, before=()):
    return pl.pallas_call(
        end_kernel,
        out_shape=(shaped((GH, GW, D), bf16), shaped((8, D), f32)),
        in_specs=[VMEM] * (5 + CALLS) + [ANY] * len(before),
        out_specs=(VMEM, VMEM),
        scratch_shapes=[pltpu.VMEM((WINDOWS * WIN, LINE, D), f32)],
        compiler_params=params(),
        cost_estimate=pl.CostEstimate(flops=8_000_000_000, bytes_accessed=17_000_000, transcendentals=0),
        name="end",
    )(images, gbr, one, two, vec, *gpacked, *before)


def pack(eight, up_bias, weight):
    return pl.pallas_call(
        pack_kernel,
        out_shape=shaped((weight.shape[0], 128 + 2 * D), bf16),
        in_specs=[VMEM] * 3,
        out_specs=VMEM,
        compiler_params=params(),
        name="pack",
    )(eight, up_bias, weight)


def one_hot_keys(flip):
    token = np.arange(TOK)
    row, col = token // LINE, token % LINE
    lane = np.arange(128)
    group, local = lane // 32, lane % 32
    hot = []
    for head in range(2):
        mine = (group % 2 == head)[None, :]
        value = ((local[None, :] == row[:, None]) & (local < WIN)[None, :]) | (
            (local[None, :] - 16 == (13 - col if flip else col)[:, None]) & (col < WIN)[:, None]
        )
        value = np.where(mine & value, 1.0, 0.0)
        value[:, 14] = np.where(col >= WIN, -1e30, 0.0)
        hot.append(value)
    return jnp.asarray(np.stack(hot), dtype=bf16)


def table_grads(total):
    rows = total[:128]
    cols = jnp.roll(total[128:], -16, axis=0)

    def pick(part):
        part = part.reshape(4, 32, 2, HD)
        value = part[0, :, 0] + part[1, :, 1] + part[2, :, 0] + part[3, :, 1]
        return value[:27]

    return pick(rows)[::-1], pick(cols)


AXES = ("dp", "fsdp")


class Exchange:
    def __init__(self, dp, fsdp):
        self.count = dp * fsdp
        self.bits = []
        bit = self.count // 2
        while bit:
            self.bits.append(bit)
            bit //= 2
        place = lax.axis_index(AXES).astype(jnp.int32)
        self.place = place
        self.mine = [(place >> (bit.bit_length() - 1)) & 1 for bit in self.bits]
        self.places = jnp.stack(self.mine)
        last = len(self.bits) - 1
        low = list(range(last - 1, 1, -1))
        self.orders = ([0, last] + low, [last, 0] + low)

    def swap(self, value, at):
        bit = self.bits[at]
        return lax.ppermute(value, AXES, [(i, i ^ bit) for i in range(self.count)])

    def spread(self, value):
        return value.reshape((1,) * len(self.bits) + value.shape)

    def join(self, value, at, flag=None):
        other = self.swap(value, at)
        mine = self.mine[at] if flag is None else self.mine[at] + flag[0]
        return jnp.where(
            mine == 0, jnp.concatenate([value, other], axis=at), jnp.concatenate([other, value], axis=at)
        )

    def total_round(self, value, ats, flag):
        value = value + flag[0].astype(f32)
        masks = [self.bits[at] for at in ats]
        move = lambda mask: lax.ppermute(value, AXES, [(i, i ^ mask) for i in range(self.count)])
        if len(masks) == 1:
            return value + move(masks[0])
        return (value + move(masks[0])) + (move(masks[1]) + move(masks[0] | masks[1]))

    def tie(self, values, before):
        count = len(values)

        def kernel(*refs):
            pass

        return pl.pallas_call(
            kernel,
            out_shape=tuple(shaped(v.shape, v.dtype) for v in values),
            in_specs=[ANY] * (count + len(before)),
            out_specs=(ANY,) * count,
            input_output_aliases={i: i for i in range(count)},
            name="tie",
        )(*values, *before)

    def flat(self, value):
        return value.reshape((self.count * value.shape[-2], value.shape[-1]))

    def cut(self, keep, send):
        rows, columns = keep.shape
        shape = (2, 1) + (2,) * (len(self.bits) - 2) + (2 * rows // self.count, columns)
        return keep.reshape(shape), self.swap(send, 1).reshape(shape)

    def narrow(self, parts, before=()):
        shapes, operands, specs, outs, out_specs = [], [], [], [], []
        for (stay, recv), at, half in parts:
            shape = stay.shape
            rows = int(np.prod(shape[at + 1 : -1]))
            lead = int(np.prod(shape[:at]))
            columns = shape[-1] if half is None else shape[-1] // 2
            block = (lead, 2, rows, columns)
            for array in (stay, recv):
                operands.append(array.reshape(lead, 2, rows, shape[-1]))
                specs.append(pl.BlockSpec(block, lambda i, c=half or 0: (0, 0, 0, c)))
            for kind in (f32, bf16):
                outs.append(shaped((lead, rows, columns), kind))
                out_specs.append(whole((lead, rows, columns)))
            shapes.append(shape[:at] + (1,) + shape[at + 1 : -1] + (columns,))
        count = len(parts)
        ats = [at for _, at, _ in parts]

        def kernel(mine_ref, *refs):
            results = refs[-2 * count - 1 : -1]
            refs[-1][0] = 0
            for i, at in enumerate(ats):
                mine = mine_ref[at]
                first, second = refs[2 * i], refs[2 * i + 1]
                for ref, place in ((results[2 * i], mine), (results[2 * i + 1], 1 - mine)):
                    total = first[:, place].astype(f32) + second[:, place].astype(f32)
                    ref[...] = total.astype(ref.dtype)

        size = sum(int(np.prod(o.shape)) for o in operands)
        got = pl.pallas_call(
            kernel,
            grid=(1,),
            out_shape=tuple(outs) + (flag_shape,),
            in_specs=[SMEM] + specs + [ANY] * len(before),
            out_specs=tuple(out_specs) + (FLAG,),
            compiler_params=params(1),
            cost_estimate=pl.CostEstimate(flops=size, bytes_accessed=4 * size, transcendentals=0),
            name="narrow",
        )(self.places, *operands, *before)
        results = []
        for i, at in enumerate(ats):
            stay, leave = got[2 * i].reshape(shapes[i]), got[2 * i + 1].reshape(shapes[i])
            results.append((stay, self.swap(leave, at)))
        return results, [got[-1]]

    def close(self, part):
        total = part[0].astype(f32) + part[1].astype(f32)
        return total.reshape(total.shape[-2:])

def local(
    dp,
    fsdp,
    images,
    grad_out,
    box_rows,
    box_cols,
    box_valid,
    box_count,
    in_weight,
    query_bias,
    value_bias,
    out_weight,
    out_bias,
    first_gain,
    first_shift,
    second_gain,
    second_shift,
    up_weight,
    up_bias,
    down_weight,
    down_bias,
    row_table,
    col_table,
):
    links = Exchange(dp, fsdp)
    image = images[0]
    core = (lax.axis_index("dp") & 1).astype(jnp.int32).reshape(1)
    hot = one_hot_keys(False)
    hot_back = one_hot_keys(True)
    eight = jnp.stack(
        [query_bias, value_bias, out_bias, first_gain, first_shift, second_gain, second_shift, down_bias]
    )
    first, second = links.orders[0][::-1], links.orders[1][::-1]
    last = len(first)
    two = links.spread(jnp.concatenate([in_weight[:, 2 * D :], out_weight], axis=1))
    one = links.spread(pack(eight, up_bias[None], in_weight))
    feed_weights = lax.all_gather(pack_feed(up_weight, down_weight), AXES, axis=0, tiled=True)
    for step in range(last - 2):
        two = links.join(two, second[step])
        one = links.join(one, first[step])
    cot, gupd, table, table_back, flag = weigh(
        box_count, grad_out[0], box_rows[0], box_cols[0], box_valid.reshape(NBOX, 1), row_table, col_table, [two, one]
    )
    two = links.join(two, second[last - 2], flag)
    one = links.join(one, first[last - 2], flag)
    unit, flag = begin(image, [two, one])
    unit = unit.reshape(WINDOWS * TOK, D)
    two = links.join(two, second[last - 1], flag)
    one = links.join(one, first[last - 1], flag)
    halves = [h.reshape(2, D // 4, -1) for h in (one, two, links.swap(one, 1), links.swap(two, 1))]

    ahead = [forward(0, unit, [links.places] + halves, table, hot)]
    weights = one, two = ahead[0][7:]
    ahead += [forward(call, unit, weights, table, hot) for call in range(1, CALLS)]
    vec = ahead[0][5]
    lines = (WINDOWS // CALLS * WIN, LINE, D)
    block_out, gbr, gup_k, gup_s, gdown_k, gdown_s, gupb, sums2 = middle(
        core, image, cot, gupd, vec, feed_weights, [a[4].reshape(lines) for a in ahead], [a[3] for a in ahead]
    )

    first, second = links.orders
    gbr_flat = gbr.reshape(WINDOWS * TOK, D)
    feed = [links.cut(gup_k, gup_s), links.cut(gdown_k, gdown_s)]
    back = []
    flag = []
    for call, (_, packed, soft, att) in enumerate([a[:4] for a in ahead]):
        back.append(backward(call, packed, soft, att, gbr_flat, two, table_back, hot_back, flag))
        flag = [back[-1][3]]
        if call == 0:
            feed, flag = links.narrow(list(zip(feed, (first[0], second[0]), (None, None))), flag)
    gin_k, gin_s, flag = attention_weights(core, [(b[0], a[0]) for a, b in zip(ahead, back)], flag)
    feed, flag = links.narrow(list(zip(feed, (first[1], second[1]), (None, None))), [flag])
    gin = links.cut(gin_k, links.tie([gin_s], flag)[0])
    image_grad, sums1 = end(image, gbr, one, two, vec, [b[0] for b in back], flag)
    gbias = sum(b[1] for b in back)
    row_grad, col_grad = table_grads(sum(b[2] for b in back))
    tables = jnp.concatenate([row_grad, col_grad, jnp.zeros((6, HD), f32)], axis=0).reshape(5, D)
    vectors = jnp.concatenate(
        [gbias[:2], sums2[2:3], sums1[:2], sums2[:2], sums2[3:4], gupb[:4], tables, jnp.zeros((7, D), f32)], axis=0
    )
    gin = [(gin, first[0], 0), (gin, second[0], 1)]
    before = [sums1]
    rounds = [first[0], 1] + first[1:]
    rounds = [rounds[i : i + 2] for i in range(0, len(rounds), 2)]
    for step in range(last):
        parts = list(gin)
        if step + 2 < last:
            parts += list(zip(feed, (first[step + 2], second[step + 2]), (None, None)))
        done, before = links.narrow(parts, before)
        if step + 1 < last:
            gin = list(zip(done[:2], (first[step + 1], second[step + 1]), (None, None)))
        feed = done[2:] or feed
        if step < len(rounds):
            vectors = links.total_round(vectors, rounds[step], before[0])
    gin = jnp.concatenate([links.close(g) for g in done[:2]], axis=1)
    gup, gout, gdown = unpack_feed(*feed)
    own = in_weight.shape[0]
    out = lax.dynamic_slice(vectors, (0, links.place * own), (12, own))
    tables = vectors[12:17].reshape(60, HD)
    row_grad, col_grad = tables[:27], tables[27:54]
    return (
        block_out[None],
        image_grad[None],
        gin,
        out[0],
        out[1],
        gout,
        out[2],
        out[3],
        out[4],
        out[5],
        out[6],
        gup,
        out[8:].reshape(-1),
        gdown,
        out[7],
        row_grad,
        col_grad,
    )


def solution(mesh):
    rows = P(AXES)
    dp, fsdp = mesh.shape["dp"], mesh.shape["fsdp"]
    return jax.shard_map(
        lambda *args: local(dp, fsdp, *args),
        mesh=mesh,
        in_specs=(rows,) * 19 + (P(), P()),
        out_specs=(rows,) * 15 + (P(), P()),
        check_vma=False,
    )
```

time: 662 us -> 378 us (0.57)
  waiting for transfers between devices: 405 us -> 50.6 us
  Pallas kernels: 155 us -> 226 us
  blocking collectives: 40.3 us -> 0 us
  starting transfers between devices: 0.5 us -> 39.4 us
  local copies, waits for them, and re-layouts: 31 us -> 20.1 us
    reduce_scatter x3 -> x0, waiting for transfers between devices: 265 us -> none  [scatter(): return lax.psum_scatter(x, AXES, scatter_dimension=0, tiled=True)]
    all_gather x3 -> x1, waiting for transfers between devices: 138 us -> 0.01 us  [local(): lax.all_gather(pack_feed(up_weight, down_weight), AXES, axis=0, tiled=True)]
    pallas_call x4 -> x19, Pallas kernels: 137 us -> 207 us  [the longest x1 68.9 us: middle(): pl.pallas_call(middle_kernel, grid=(steps + 1,), out_shape=(shaped((GH, G...]
    ppermute x0 -> x36, waiting for transfers between devices: none -> 50.6 us  [the longest x29 50.5 us: swap(): return lax.ppermute(value, AXES, [(i, i ^ bit) for i in range(self.count)])]
    psum x1 -> x0, blocking collectives: 40.3 us -> none  [local(): flat = lax.psum(flat, AXES)]
    ppermute x0 -> x36, starting transfers between devices: none -> 39.3 us  [the longest x29 30 us: swap(): return lax.ppermute(value, AXES, [(i, i ^ bit) for i in range(self.count)])]
    slice x15 -> x8, local copies, waits for them, and re-layouts: 13.7 us -> 4.51 us  [the longest x1 0.82 us: local(): sums2[3:4]]
    select_n x0 -> x10, other arithmetic: none -> 7.26 us  [join(): jnp.where(mine == 0, jnp.concatenate([value, other], axis=at), jnp.concat...]
  transfers between devices with their start and end apart: 6 -> 37, of which waited for: 6 -> 15; matrix products, arithmetic and copies ran while one was open for 5% -> 7% of each run, Pallas kernels for 8% -> 35%
where the time goes in v2:
time: 378 us; the launch traced here: 373 us
  Pallas kernels  226 us (60%)
  waiting for transfers between devices  50.6 us (13%)
  starting transfers between devices  39.4 us (10%)
  between operations  20.2 us (5%)
  local copies, waits for them, and re-layouts  20.1 us (5%)
  other arithmetic  16 us (4%)
    pallas_call x1, Pallas kernels, middle(): pl.pallas_call(middle_kernel, grid=(steps + 1,), out_shape=(shaped((GH, G...  68.9 us
    ppermute x29, waiting for transfers between devices, swap(): return lax.ppermute(value, AXES, [(i, i ^ bit) for i in range(self.count)])  50.5 us
    pallas_call x3, Pallas kernels, backward(): pl.pallas_call(backward_kernel, grid=(each,), out_shape=(shaped((each * T...  41.4 us
    pallas_call x3, Pallas kernels, forward(): pl.pallas_call(functools.partial(forward_kernel, call), grid=(each,), out...  39.6 us
    pallas_call x6, Pallas kernels, narrow(): pl.pallas_call(kernel, grid=(1,), out_shape=tuple(outs) + (flag_shape,),...  31.2 us
    ppermute x29, starting transfers between devices, swap(): return lax.ppermute(value, AXES, [(i, i ^ bit) for i in range(self.count)])  30 us
    pallas_call x1, Pallas kernels, end(): pl.pallas_call(end_kernel, out_shape=(shaped((GH, GW, D), bf16), shaped((...  14.6 us
    pallas_call x1, Pallas kernels, attention_weights(): pl.pallas_call(attention_weights_kernel, grid=(1,), out_shape=(shaped((D...  13.9 us
  transfers between devices with their start and end apart: 37, of which 15 were waited for; matrix products, arithmetic and copies ran while one was open for 7% of the time, Pallas kernels for 35%

profile of v2, /device:TPU:0, one launch (start us, length us, event | category | flops | bytes accessed | tf_op | source)
XLA Modules:
  0.0 372.6 jit_solution(15924424389118954887)
XLA Ops:
  7.3 1.9 pack_feed.1
  10.8 4.1 %collective-permute-start = (bf16[1,1,1,1,1,24,1536]{6,5,4,3,2,1,0:T(8,128)(2,1)S(1)}, bf16[1,1,1,1,1,24,1536]{6,5,4,3,2,1,0:T(8,128)(2,1)S(1)}, u32[]{:S(2)}, u32[]{:S(2)}) collective-permute-start(bf16[1,1,1,1,1,24,1536]{6,5,4,3,2,1,0:T(8,128)(2,1)S(1)} %get-tuple-element.227), channel_id=1, source_target_pairs={{0,4},{1,5},{2,6},{3,7},{4,0},{5,1},{6,2},{7,3},{8,12},{9,13},{10,... | collective-permute-start | bytes 221192 | tf_op jit(solution)/shard_map/ppermute | solution.py:770
  14.9 1.4 stack.53.eight_ref
  16.3 1.7 pack.1
  21.1 2.0 collective-permute-start.1
  23.1 1.8 collective-permute-done.2
  24.9 1.0 fusion.7
  26.3 4.5 %collective-permute-done.1 = bf16[1,1,2,1,1,24,1536]{6,5,2,4,3,1,0:T(8,128)(2,1)S(1)} collective-permute-done((bf16[1,1,2,1,1,24,1536]{6,5,2,4,3,1,0:T(8,128)(2,1)S(1)}, bf16[1,1,2,1,1,24,1536]{6,5,2,4,3,1,0:T(8,128)(2,1)S(1)}, u32[]{:S(2)}, u32[]{:S(2)}) %collective-permute-start.1) | collective-permute-done | bytes 147488 | tf_op jit(solution)/shard_map/ppermute | solution.py:770
  31.6 2.0 collective-permute-start.4
  34.3 1.3 collective-permute-done.3
  35.7 1.6 collective-permute-start.5
  38.1 4.9 %weigh.1 = (f32[992,768]{1,0:T(8,128)}, bf16[992,768]{1,0:T(8,128)(2,1)}, bf16[128,256]{1,0:T(8,128)(2,1)}, bf16[128,256]{1,0:T(8,128)(2,1)}, s32[1]{0:T(128)}) custom-call(s32[1]{0:T(128)S(6)} %copy.93.count_ref, bf16[26,38,768]{2,1,0:T(8,128)(2,1)} %bitcast.191, s32[300,2]{1,0:T(8,128)} %bitcast.209, s32[300,2]{1,0:T(8,128)} %bitcast.210, ...), custom_call_target="tpu_custom_call" | custom-call | flops 30000000 | bytes 6000000 | tf_op jit(solution)/shard_map/weigh/pallas_call | solution.py:543
  46.0 1.6 collective-permute-start.6
  48.3 1.2 fusion.6
  49.5 5.0 %begin.1 = (f32[84,16,768]{2,1,0:T(8,128)}, s32[1]{0:T(128)}) custom-call(bf16[26,38,768]{2,1,0:T(8,128)(2,1)} %bitcast.192, bf16[2,1,2,2,1,24,1536]{6,5,4,3,2,1,0:T(8,128)(2,1)} %copy-done.1, bf16[1,1,2,2,2,24,1664]{6,5,4,3,2,1,0:T(8,128)(2,1)} %copy-done.4), custom_call_target="tpu_custom_call" | custom-call | flops 30000000 | bytes 6000000 | tf_op jit(solution)/shard_map/begin/pallas_call | solution.py:531
  55.8 1.3 fusion.4
  57.2 6.0 %collective-permute-done.6 = bf16[1,1,2,2,2,24,1664]{6,5,4,3,2,1,0:T(8,128)(2,1)S(1)} collective-permute-done((bf16[1,1,2,2,2,24,1664]{6,5,4,3,2,1,0:T(8,128)(2,1)S(1)}, bf16[1,1,2,2,2,24,1664]{6,5,4,3,2,1,0:T(8,128)(2,1)S(1)}, u32[]{:S(2)}, u32[]{:S(2)}) %collective-permute-start.6) | collective-permute-done | bytes 639008 | tf_op jit(solution)/shard_map/ppermute | solution.py:770
  63.2 1.3 maximum_select_fusion.1
  64.5 2.0 collective-permute-done.7
  66.5 2.5 fusion.1
  69.6 1.3 maximum_select_fusion.one_ref
  70.9 1.1 collective-permute-done.9
  72.0 15.0 %attend.3 = (bf16[448,768]{1,0:T(8,128)(2,1)}, bf16[448,2304]{1,0:T(8,128)(2,1)}, bf16[24,224,224]{2,1,0:T(8,128)(2,1)}, bf16[448,768]{1,0:T(8,128)(2,1)}, f32[4...) custom-call(s32[5]{0:T(128)} %stack.59.unit_ref.mine_ref, ...), custom_call_target="tpu_custom_call" | custom-call | flops 10000000000 | bytes 9000000 | tf_op jit(solution)/shard_map/attend/pallas_call | solution.py:572
  87.0 12.3 %attend.5 = (bf16[448,768]{1,0:T(8,128)(2,1)}, bf16[448,2304]{1,0:T(8,128)(2,1)}, bf16[24,224,224]{2,1,0:T(8,128)(2,1)}, bf16[448,768]{1,0:T(8,128)(2,1)}, f32[4...) custom-call(f32[1344,768]{1,0:T(8,128)} %bitcast.248, bf16[768,1664]{1,0:T(8,128)(2,1)} %get-tuple-element.115.one_ref, ...), custom_call_target="tpu_custom_call" | custom-call | flops 10000000000 | bytes 9000000 | tf_op jit(solution)/shard_map/attend/pallas_call | solution.py:572
  99.3 12.3 %attend.4 = (bf16[448,768]{1,0:T(8,128)(2,1)}, bf16[448,2304]{1,0:T(8,128)(2,1)}, bf16[24,224,224]{2,1,0:T(8,128)(2,1)}, bf16[448,768]{1,0:T(8,128)(2,1)}, f32[4...) custom-call(f32[1344,768]{1,0:T(8,128)} %bitcast.249, bf16[768,1664]{1,0:T(8,128)(2,1)} %get-tuple-element.115.one_ref, ...), custom_call_target="tpu_custom_call" | custom-call | flops 10000000000 | bytes 9000000 | tf_op jit(solution)/shard_map/attend/pallas_call | solution.py:572
  111.6 68.9 %feed.1 = (bf16[26,38,768]{2,1,0:T(8,128)(2,1)}, bf16[84,16,768]{2,1,0:T(8,128)(2,1)}, bf16[384,3840]{1,0:T(8,128)(2,1)}, bf16[384,3840]{1,0:T(8,128)(2,1)}, bf1...) custom-call(s32[1]{0:T(128)} %bitcast.core_ref, ...), custom_call_target="tpu_custom_call" | custom-call | flops 49999998976 | bytes 36000000 | tf_op jit(solution)/shard_map/feed/pallas_call | solution.py:602
  183.4 13.4 %attend_back.3 = (bf16[448,2304]{1,0:T(8,128)(2,1)}, f32[8,768]{1,0:T(8,128)}, f32[256,128]{1,0:T(8,128)}, s32[1]{0:T(128)}) custom-call(bf16[448,2304]{1,0:T(8,128)(2,1)} %get-tuple-element.124.packed_ref, bf16[24,224,224]{2,1,0:T(8,128)(2,1)} %get-tuple-element.125.soft_ref, bf16[448,768]{1,0:T(8,128)(2,1)} %get-tuple-element.119.refs_3_.att_ref, ...), custom_call_target="tpu_custom_call" | custom-call | flops 12000000000 | bytes 9000000 | tf_op jit(solution)/shard_map/attend_back/pallas_call | solution.py:653
  196.9 1.6 copy-done.3
  198.5 9.0 %narrow.6 = (f32[1,192,3840]{2,1,0:T(8,128)}, bf16[1,192,3840]{2,1,0:T(8,128)(2,1)}, f32[8,24,3072]{2,1,0:T(8,128)}, bf16[8,24,3072]{2,1,0:T(8,128)(2,1)}, s32[1]{0:T(128)}) custom-call(s32[5]{0:T(128)} %stack.59.unit_ref.mine_ref, bf16[1,2,192,3840]{3,2,1,0:T(8,128)(2,1)} %bitcast.181, bf16[1,2,192,3840]{3,2,1,0:T(8,128)(2,1)} %bitcast.182, ...), custom_call_target="tpu_custom_call" | custom-call | flops 5308416 | bytes 21233664 | tf_op jit(solution)/shard_map/narrow/pallas_call | solution.py:842
  207.5 1.7 collective-permute-start.12
  210.0 13.9 %attend_back.4 = (bf16[448,2304]{1,0:T(8,128)(2,1)}, f32[8,768]{1,0:T(8,128)}, f32[256,128]{1,0:T(8,128)}, s32[1]{0:T(128)}) custom-call(bf16[448,2304]{1,0:T(8,128)(2,1)} %get-tuple-element.128.packed_ref, bf16[24,224,224]{2,1,0:T(8,128)(2,1)} %get-tuple-element.129.soft_ref, bf16[448,768]{1,0:T(8,128)(2,1)} %get-tuple-element.120.refs_4_.att_ref, ...), custom_call_target="tpu_custom_call" | custom-call | flops 12000000000 | bytes 9000000 | tf_op jit(solution)/shard_map/attend_back/pallas_call | solution.py:653
  223.9 14.1 %attend_back.5 = (bf16[448,2304]{1,0:T(8,128)(2,1)}, f32[8,768]{1,0:T(8,128)}, f32[256,128]{1,0:T(8,128)}, s32[1]{0:T(128)}) custom-call(bf16[448,2304]{1,0:T(8,128)(2,1)} %get-tuple-element.137.packed_ref, bf16[24,224,224]{2,1,0:T(8,128)(2,1)} %get-tuple-element.138.soft_ref, bf16[448,768]{1,0:T(8,128)(2,1)} %get-tuple-element.121.refs_5_.att_ref, ...), custom_call_target="tpu_custom_call" | custom-call | flops 12000000000 | bytes 9000000 | tf_op jit(solution)/shard_map/attend_back/pallas_call | solution.py:653
  238.0 0.9 add_add_fusion
  239.1 13.9 %attend_weights.1 = (bf16[384,2304]{1,0:T(8,128)(2,1)}, bf16[384,2304]{1,0:T(8,128)(2,1)}, s32[1]{0:T(128)}) custom-call(s32[1]{0:T(128)} %bitcast.core_ref, bf16[448,2304]{1,0:T(8,128)(2,1)} %get-tuple-element.127.refs_0_, bf16[448,768]{1,0:T(8,128)(2,1)} %get-tuple-element.145.refs_1_, bf16[448,2304]{1,0:T(8,128)(2,1)} %get-tuple-element.136.refs_2_.refs_1_, ...), custom_call_target="tpu_custom_call" | custom-call | flops 24999999488 | bytes 18000000 | tf_op jit(solution)/shard_map/attend_weights/pallas_call | solution.py:683
  253.1 1.0 copy-done.9
  254.6 6.3 %narrow.7 = (f32[4,24,3840]{2,1,0:T(8,128)}, bf16[4,24,3840]{2,1,0:T(8,128)(2,1)}, f32[1,96,3072]{2,1,0:T(8,128)}, bf16[1,96,3072]{2,1,0:T(8,128)(2,1)}, s32[1]{0:T(128)}) custom-call(s32[5]{0:T(128)} %stack.59.unit_ref.mine_ref, f32[4,2,24,3840]{3,2,1,0:T(8,128)} %bitcast.180, bf16[4,2,24,3840]{3,2,1,0:T(8,128)(2,1)} %bitcast.196, ...), custom_call_target="tpu_custom_call" | custom-call | flops 2654208 | bytes 10616832 | tf_op jit(solution)/shard_map/narrow/pallas_call | solution.py:842
  262.8 1.3 collective-permute-start.15
  264.4 14.6 %end.1 = (bf16[26,38,768]{2,1,0:T(8,128)(2,1)}, f32[8,768]{1,0:T(8,128)}) custom-call(bf16[26,38,768]{2,1,0:T(8,128)(2,1)} %bitcast.194, bf16[84,16,768]{2,1,0:T(8,128)(2,1)} %get-tuple-element.123.gbr_ref, bf16[768,1664]{1,0:T(8,128)(2,1)} %get-tuple-element.115.one_ref, bf16[768,1536]{1,0:T(8,128)(2,1)} %get-tuple-element.116.two_ref, ...), custom_call_target="tpu_custom_call" | custom-call | flops 8000000000 | bytes 17000000 | tf_op jit(solution)/shard_map/end/pallas_call | solution.py:697
  279.7 2.2 collective-permute-done.15
  281.9 0.9 copy-done.11
  283.4 5.8 %narrow.8 = (f32[1,192,1152]{2,1,0:T(8,128)}, bf16[1,192,1152]{2,1,0:T(8,128)(2,1)}, f32[8,24,1152]{2,1,0:T(8,128)}, bf16[8,24,1152]{2,1,0:T(8,128)(2,1)}, f32[2...) custom-call(s32[5]{0:T(128)} %stack.59.unit_ref.mine_ref, ...), custom_call_target="tpu_custom_call" | custom-call | flops 4866048 | bytes 19464192 | tf_op jit(solution)/shard_map/narrow/pallas_call | solution.py:842
  289.8 1.1 collective-permute-start.18
  290.9 1.6 collective-permute-start.19
  294.6 1.7 collective-permute-start.27
  296.4 10.7 %collective-permute-done.20 = bf16[1,1,2,1,1,24,3072]{6,5,2,4,3,1,0:T(8,128)(2,1)S(1)} collective-permute-done((bf16[1,1,2,1,1,24,3072]{6,5,2,4,3,1,0:T(8,128)(2,1)}, bf16[1,1,2,1,1,24,3072]{6,5,2,4,3,1,0:T(8,128)(2,1)S(1)}, u32[]{:S(2)}, u32[]{:S(2)}) %collective-permute-start.20) | collective-permute-done | bytes 294944 | tf_op jit(solution)/shard_map/ppermute | solution.py:770
  307.1 1.8 collective-permute-start.29
  309.8 4.6 %narrow.9 = (f32[4,24,1152]{2,1,0:T(8,128)}, bf16[4,24,1152]{2,1,0:T(8,128)(2,1)}, f32[1,96,1152]{2,1,0:T(8,128)}, bf16[1,96,1152]{2,1,0:T(8,128)(2,1)}, f32[1,2...) custom-call(s32[5]{0:T(128)} %stack.59.unit_ref.mine_ref, ...), custom_call_target="tpu_custom_call" | custom-call | flops 1548288 | bytes 6193152 | tf_op jit(solution)/shard_map/narrow/pallas_call | solution.py:842
  316.5 1.1 collective-permute-start.30
  317.6 1.6 collective-permute-start.31
  320.0 5.0 %collective-permute-done.21 = bf16[1,1,2,2,1,24,1152]{6,5,3,2,4,1,0:T(8,128)(2,1)S(1)} collective-permute-done((bf16[1,1,2,2,1,24,1152]{6,5,3,2,4,1,0:T(8,128)(2,1)}, bf16[1,1,2,2,1,24,1152]{6,5,3,2,4,1,0:T(8,128)(2,1)S(1)}, u32[]{:S(2)}, u32[]{:S(2)}) %collective-permute-start.21) | collective-permute-done | bytes 221216 | tf_op jit(solution)/shard_map/ppermute | solution.py:770
  325.1 2.4 collective-permute-start.34
  328.2 2.9 narrow.10
  331.9 2.3 collective-permute-start.33
  334.2 8.1 %collective-permute-done.35 = bf16[1,1,1,1,1,24,3072]{6,5,4,3,2,1,0:T(8,128)(2,1)S(1)} collective-permute-done((bf16[1,1,1,1,1,24,3072]{6,5,4,3,2,1,0:T(8,128)(2,1)}, bf16[1,1,1,1,1,24,3072]{6,5,4,3,2,1,0:T(8,128)(2,1)S(1)}, u32[]{:S(2)}, u32[]{:S(2)}) %collective-permute-start.35) | collective-permute-done | bytes 147488 | tf_op jit(solution)/shard_map/ppermute | solution.py:770
  343.0 2.5 unpack_feed.1
  346.0 1.6 collective-permute-start.24
  348.3 2.0 collective-permute-done.23
  350.3 1.2 collective-permute-done.24
  352.1 2.6 narrow.11
  354.7 2.6 collective-permute-start.25
  359.0 2.5 collective-permute-done.25
  361.4 0.9 fusion.10
  362.4 1.5 collective-permute-done.26
  363.9 0.9 fusion.9
  (160 shorter events, 28.5 us)
Async XLA Ops:
  7.2 10.8 %copy-start.26 = (s32[1,300,2]{1,2,0:T(2,128)S(1)}, s32[1,300,2]{1,2,0:T(2,128)}, u32[]{:S(2)}) copy-start(s32[1,300,2]{1,2,0:T(2,128)} %param.25) | copy-start | bytes 7204
  7.2 11.6 %copy-start.27 = (s32[1,300,2]{1,2,0:T(2,128)S(1)}, s32[1,300,2]{1,2,0:T(2,128)}, u32[]{:S(2)}) copy-start(s32[1,300,2]{1,2,0:T(2,128)} %param.26) | copy-start | bytes 7204
  7.2 12.4 %copy-start.28 = (s32[1,300]{1,0:T(1,128)S(1)}, s32[1,300]{1,0:T(1,128)}, u32[]{:S(2)}) copy-start(s32[1,300]{1,0:T(1,128)} %param.27) | copy-start | bytes 3604
  7.2 104.4 %all-gather.2.cloned.1.call-start = ((), (), s32[]{:S(2)}) async-start(), calls=%async_computation | async-start | bytes 9732096 | tf_op jit(solution)/shard_map/all_gather | solution.py:899
  10.8 10.3 %collective-permute-start = (bf16[1,1,1,1,1,24,1536]{6,5,4,3,2,1,0:T(8,128)(2,1)S(1)}, bf16[1,1,1,1,1,24,1536]{6,5,4,3,2,1,0:T(8,128)(2,1)S(1)}, u32[]{:S(2)}, u32[]{:S(2)}) collective-permute-start(bf16[1,1,1,1,1,24,1536]{6,5,4,3,2,1,0:T(8,128)(2,1)S(1)} %get-tuple-element.227), channel_id=1, source_target_pairs={{0,4},{1,5},{2,6},{3,7},{4,0},{5,1},{6,2},{7,3},{8,12},{9,13},{10,... | collective-permute-start | bytes 221192 | tf_op jit(solution)/shard_map/ppermute | solution.py:770
  18.0 8.3 %copy-start.12 = (bf16[24,1664]{1,0:T(8,128)(2,1)S(1)}, bf16[24,1664]{1,0:T(8,128)(2,1)}, u32[]{:S(2)}) copy-start(bf16[24,1664]{1,0:T(8,128)(2,1)} %pack.1) | copy-start | bytes 239620
  18.0 6.9 %collective-permute-start.2 = (bf16[1,1,1,1,1,24,1664]{6,5,4,3,2,1,0:T(8,128)(2,1)}, bf16[1,1,1,1,1,24,1664]{6,5,4,3,2,1,0:T(8,128)(2,1)S(1)}, u32[]{:S(2)}, u32[]{:S(2)}) collective-permute-start(bf16[1,1,1,1,1,24,1664]{6,5,4,3,2,1,0:T(8,128)(2,1)} %bitcast.206), channel_id=1, source_target_pairs={{0,4},{1,5},{2,6},{3,7},{4,0},{5,1},{6,2},{7,3},{8,12},{9,13},{10,... | collective-permute-start | bytes 239624 | tf_op jit(solution)/shard_map/ppermute | solution.py:770
  21.1 9.7 %collective-permute-start.1 = (bf16[1,1,2,1,1,24,1536]{6,5,2,4,3,1,0:T(8,128)(2,1)S(1)}, bf16[1,1,2,1,1,24,1536]{6,5,2,4,3,1,0:T(8,128)(2,1)S(1)}, u32[]{:S(2)}, u32[]{:S(2)}) collective-permute-start(bf16[1,1,2,1,1,24,1536]{6,5,2,4,3,1,0:T(8,128)(2,1)S(1)} %fusion.8), channel_id=1, source_target_pairs={{0,2},{1,3},{2,0},{3,1},{4,6},{5,7},{6,4},{7,5},{8,10},{9,11},{10,... | collective-permute-start | bytes 442376 | tf_op jit(solution)/shard_map/ppermute | solution.py:770
  25.9 9.7 %collective-permute-start.3 = (bf16[1,1,2,1,1,24,1664]{6,5,2,4,3,1,0:T(8,128)(2,1)S(1)}, bf16[1,1,2,1,1,24,1664]{6,5,2,4,3,1,0:T(8,128)(2,1)S(1)}, u32[]{:S(2)}, u32[]{:S(2)}) collective-permute-start(bf16[1,1,2,1,1,24,1664]{6,5,2,4,3,1,0:T(8,128)(2,1)S(1)} %fusion.7), channel_id=1, source_target_pairs={{0,2},{1,3},{2,0},{3,1},{4,6},{5,7},{6,4},{7,5},{8,10},{9,11},{10,... | collective-permute-start | bytes 479240 | tf_op jit(solution)/shard_map/ppermute | solution.py:770
  31.6 16.0 %collective-permute-start.4 = (bf16[1,1,2,2,1,24,1536]{6,5,3,2,4,1,0:T(8,128)(2,1)S(1)}, bf16[1,1,2,2,1,24,1536]{6,5,3,2,4,1,0:T(8,128)(2,1)S(1)}, u32[]{:S(2)}, u32[]{:S(2)}) collective-permute-start(bf16[1,1,2,2,1,24,1536]{6,5,3,2,4,1,0:T(8,128)(2,1)S(1)} %copy.69), channel_id=1, source_target_pairs={{0,16},{1,17},{2,18},{3,19},{4,20},{5,21},{6,22},{7,23},{8,24},{9,... | collective-permute-start | bytes 884744 | tf_op jit(solution)/shard_map/ppermute | solution.py:770
  35.7 9.5 %collective-permute-start.5 = (bf16[1,1,2,2,1,24,1664]{6,5,2,3,4,1,0:T(8,128)(2,1)S(1)}, bf16[1,1,2,2,1,24,1664]{6,5,2,3,4,1,0:T(8,128)(2,1)S(1)}, u32[]{:S(2)}, u32[]{:S(2)}) collective-permute-start(bf16[1,1,2,2,1,24,1664]{6,5,2,3,4,1,0:T(8,128)(2,1)S(1)} %maximum_select_fusion.3), channel_id=1, source_target_pairs={{0,1},{1,0},{2,3},{3,2},{4,5},{5,4},{6,7},{7,6},{8,9},{9,8},{10,11... | collective-permute-start | bytes 958472 | tf_op jit(solution)/shard_map/ppermute | solution.py:770
  45.2 0.7 copy-start.6
  45.9 2.4 copy-start.8
  46.0 3.5 copy-start.4
  46.0 17.2 %collective-permute-start.6 = (bf16[1,1,2,2,2,24,1664]{6,5,4,3,2,1,0:T(8,128)(2,1)S(1)}, bf16[1,1,2,2,2,24,1664]{6,5,4,3,2,1,0:T(8,128)(2,1)S(1)}, u32[]{:S(2)}, u32[]{:S(2)}) collective-permute-start(bf16[1,1,2,2,2,24,1664]{6,5,4,3,2,1,0:T(8,128)(2,1)S(1)} %copy_select_fusion.refs_1_), channel_id=1, source_target_pairs={{0,16},{1,17},{2,18},{3,19},{4,20},{5,21},{6,22},{7,23},{8,24},{9,... | collective-permute-start | bytes 1916936 | tf_op jit(solution)/shard_map/ppermute | solution.py:770
  47.7 1.8 copy-start.1
  47.7 18.8 %collective-permute-start.7 = (bf16[2,1,2,2,1,24,1536]{6,5,4,3,2,1,0:T(8,128)(2,1)S(1)}, bf16[2,1,2,2,1,24,1536]{6,5,4,3,2,1,0:T(8,128)(2,1)}, u32[]{:S(2)}, u32[]{:S(2)}) collective-permute-start(bf16[2,1,2,2,1,24,1536]{6,5,4,3,2,1,0:T(8,128)(2,1)S(1)} %fusion.5.refs_0_), channel_id=1, source_target_pairs={{0,1},{1,0},{2,3},{3,2},{4,5},{5,4},{6,7},{7,6},{8,9},{9,8},{10,11... | collective-permute-start | bytes 1769480 | tf_op jit(solution)/shard_map/ppermute | solution.py:770
  49.5 6.3 %copy-start.7 = (bf16[1,1,2,2,1,24,1664]{6,5,2,3,4,1,0:T(8,128)(2,1)S(1)}, bf16[1,1,2,2,1,24,1664]{6,5,2,3,4,1,0:T(8,128)(2,1)}, u32[]{:S(2)}) copy-start(bf16[1,1,2,2,1,24,1664]{6,5,2,3,4,1,0:T(8,128)(2,1)} %copy-done.6) | copy-start | bytes 958468
  57.2 9.3 %copy-start.2 = (bf16[2,1,2,2,1,24,1536]{6,5,4,3,2,1,0:T(8,128)(2,1)S(1)}, bf16[2,1,2,2,1,24,1536]{6,5,4,3,2,1,0:T(8,128)(2,1)}, u32[]{:S(2)}) copy-start(bf16[2,1,2,2,1,24,1536]{6,5,4,3,2,1,0:T(8,128)(2,1)} %copy-done.1) | copy-start | bytes 1769476
  64.5 7.5 %collective-permute-start.8 = (bf16[2,1,2,2,2,24,1664]{6,5,4,3,2,1,0:T(8,128)(2,1)}, bf16[2,1,2,2,2,24,1664]{6,5,4,3,2,1,0:T(8,128)(2,1)}, u32[]{:S(2)}, u32[]{:S(2)}) collective-permute-start(bf16[2,1,2,2,2,24,1664]{6,5,4,3,2,1,0:T(8,128)(2,1)} %maximum_select_fusion.1), channel_id=1, source_target_pairs={{0,8},{1,9},{2,10},{3,11},{4,12},{5,13},{6,14},{7,15},{8,0},{9,1},... | collective-permute-start | bytes 3833864 | tf_op jit(solution)/shard_map/ppermute | solution.py:770
  69.0 3.0 collective-permute-start.9
  180.5 16.4 %collective-permute-start.10 = (bf16[384,3840]{1,0:T(8,128)(2,1)}, bf16[384,3840]{1,0:T(8,128)(2,1)S(1)}, u32[]{:S(2)}, u32[]{:S(2)}) collective-permute-start(bf16[384,3840]{1,0:T(8,128)(2,1)} %get-tuple-element.131), channel_id=1, source_target_pairs={{0,8},{1,9},{2,10},{3,11},{4,12},{5,13},{6,14},{7,15},{8,0},{9,1},... | collective-permute-start | bytes 8847368 | tf_op jit(solution)/shard_map/ppermute | solution.py:770
  180.7 16.1 %collective-permute-start.11 = (bf16[384,3072]{1,0:T(8,128)(2,1)}, bf16[384,3072]{1,0:T(8,128)(2,1)}, u32[]{:S(2)}, u32[]{:S(2)}) collective-permute-start(bf16[384,3072]{1,0:T(8,128)(2,1)} %get-tuple-element.133), channel_id=1, source_target_pairs={{0,8},{1,9},{2,10},{3,11},{4,12},{5,13},{6,14},{7,15},{8,0},{9,1},... | collective-permute-start | bytes 7077896 | tf_op jit(solution)/shard_map/ppermute | solution.py:770
  196.9 1.6 copy-start.3
  207.5 45.6 %collective-permute-start.12 = (bf16[1,1,2,2,2,24,3840]{6,5,4,3,2,1,0:T(8,128)(2,1)}, bf16[1,1,2,2,2,24,3840]{6,5,4,3,2,1,0:T(8,128)(2,1)S(1)}, u32[]{:S(2)}, u32[]{:S(2)}) collective-permute-start(bf16[1,1,2,2,2,24,3840]{6,5,4,3,2,1,0:T(8,128)(2,1)} %bitcast.250), channel_id=1, source_target_pairs={{0,16},{1,17},{2,18},{3,19},{4,20},{5,21},{6,22},{7,23},{8,24},{9,... | collective-permute-start | bytes 4423688 | tf_op jit(solution)/shard_map/ppermute | solution.py:770
  209.2 43.8 %collective-permute-start.13 = (bf16[2,1,2,2,1,24,3072]{6,5,3,2,0,4,1:T(8,128)(2,1)}, bf16[2,1,2,2,1,24,3072]{6,5,3,2,0,4,1:T(8,128)(2,1)S(1)}, u32[]{:S(2)}, u32[]{:S(2)}) collective-permute-start(bf16[2,1,2,2,1,24,3072]{6,5,3,2,0,4,1:T(8,128)(2,1)} %bitcast.251), channel_id=1, source_target_pairs={{0,1},{1,0},{2,3},{3,2},{4,5},{5,4},{6,7},{7,6},{8,9},{9,8},{10,11... | collective-permute-start | bytes 3538952 | tf_op jit(solution)/shard_map/ppermute | solution.py:770
  223.9 14.1 %copy-start.22 = (f32[256,128]{1,0:T(8,128)S(1)}, f32[256,128]{1,0:T(8,128)}, u32[]{:S(2)}) copy-start(f32[256,128]{1,0:T(8,128)} %get-tuple-element.187) | copy-start | bytes 393220
  223.9 14.1 %copy-start.23 = (f32[256,128]{1,0:T(8,128)S(1)}, f32[256,128]{1,0:T(8,128)}, u32[]{:S(2)}) copy-start(f32[256,128]{1,0:T(8,128)} %get-tuple-element.188) | copy-start | bytes 393220
  253.1 1.0 copy-start.9
  253.1 1.5 copy-start.5
  261.5 20.4 %collective-permute-start.14 = (bf16[384,2304]{1,0:T(8,128)(2,1)}, bf16[384,2304]{1,0:T(8,128)(2,1)S(1)}, u32[]{:S(2)}, u32[]{:S(2)}) collective-permute-start(bf16[384,2304]{1,0:T(8,128)(2,1)} %tie.1), channel_id=1, source_target_pairs={{0,8},{1,9},{2,10},{3,11},{4,12},{5,13},{6,14},{7,15},{8,0},{9,1},... | collective-permute-start | bytes 5308424 | tf_op jit(solution)/shard_map/ppermute | solution.py:770
  262.8 19.1 %collective-permute-start.15 = (bf16[1,1,2,2,1,24,3840]{6,5,3,2,4,1,0:T(8,128)(2,1)}, bf16[1,1,2,2,1,24,3840]{6,5,3,2,4,1,0:T(8,128)(2,1)S(1)}, u32[]{:S(2)}, u32[]{:S(2)}) collective-permute-start(bf16[1,1,2,2,1,24,3840]{6,5,3,2,4,1,0:T(8,128)(2,1)} %bitcast.252), channel_id=1, source_target_pairs={{0,1},{1,0},{2,3},{3,2},{4,5},{5,4},{6,7},{7,6},{8,9},{9,8},{10,11... | collective-permute-start | bytes 2211848 | tf_op jit(solution)/shard_map/ppermute | solution.py:770
  264.0 15.7 %collective-permute-start.16 = (bf16[1,1,2,2,1,24,3072]{6,5,3,2,4,1,0:T(8,128)(2,1)}, bf16[1,1,2,2,1,24,3072]{6,5,3,2,4,1,0:T(8,128)(2,1)S(1)}, u32[]{:S(2)}, u32[]{:S(2)}) collective-permute-start(bf16[1,1,2,2,1,24,3072]{6,5,3,2,4,1,0:T(8,128)(2,1)} %bitcast.253), channel_id=1, source_target_pairs={{0,16},{1,17},{2,18},{3,19},{4,20},{5,21},{6,22},{7,23},{8,24},{9,... | collective-permute-start | bytes 1769480 | tf_op jit(solution)/shard_map/ppermute | solution.py:770
  279.7 2.2 copy-start.13
  281.9 0.9 copy-start.11
  281.9 1.5 copy-start
  289.2 19.7 %collective-permute-start.17 = (bf16[1,1,2,2,2,24,1152]{6,5,4,3,2,1,0:T(8,128)(2,1)}, bf16[1,1,2,2,2,24,1152]{6,5,4,3,2,1,0:T(8,128)(2,1)S(1)}, u32[]{:S(2)}, u32[]{:S(2)}) collective-permute-start(bf16[1,1,2,2,2,24,1152]{6,5,4,3,2,1,0:T(8,128)(2,1)} %bitcast.255), channel_id=1, source_target_pairs={{0,16},{1,17},{2,18},{3,19},{4,20},{5,21},{6,22},{7,23},{8,24},{9,... | collective-permute-start | bytes 1327112 | tf_op jit(solution)/shard_map/ppermute | solution.py:770
  289.8 19.0 %collective-permute-start.18 = (bf16[2,1,2,2,1,24,1152]{6,5,3,2,0,4,1:T(8,128)(2,1)}, bf16[2,1,2,2,1,24,1152]{6,5,3,2,0,4,1:T(8,128)(2,1)S(1)}, u32[]{:S(2)}, u32[]{:S(2)}) collective-permute-start(bf16[2,1,2,2,1,24,1152]{6,5,3,2,0,4,1:T(8,128)(2,1)} %bitcast.254), channel_id=1, source_target_pairs={{0,1},{1,0},{2,3},{3,2},{4,5},{5,4},{6,7},{7,6},{8,9},{9,8},{10,11... | collective-permute-start | bytes 1327112 | tf_op jit(solution)/shard_map/ppermute | solution.py:770
  290.9 16.2 %collective-permute-start.19 = (bf16[1,1,2,1,1,24,3840]{6,5,2,4,3,1,0:T(8,128)(2,1)}, bf16[1,1,2,1,1,24,3840]{6,5,2,4,3,1,0:T(8,128)(2,1)S(1)}, u32[]{:S(2)}, u32[]{:S(2)}) collective-permute-start(bf16[1,1,2,1,1,24,3840]{6,5,2,4,3,1,0:T(8,128)(2,1)} %bitcast.256), channel_id=1, source_target_pairs={{0,2},{1,3},{2,0},{3,1},{4,6},{5,7},{6,4},{7,5},{8,10},{9,11},{10,... | collective-permute-start | bytes 1105928 | tf_op jit(solution)/shard_map/ppermute | solution.py:770
  292.5 14.5 %collective-permute-start.20 = (bf16[1,1,2,1,1,24,3072]{6,5,2,4,3,1,0:T(8,128)(2,1)}, bf16[1,1,2,1,1,24,3072]{6,5,2,4,3,1,0:T(8,128)(2,1)S(1)}, u32[]{:S(2)}, u32[]{:S(2)}) collective-permute-start(bf16[1,1,2,1,1,24,3072]{6,5,2,4,3,1,0:T(8,128)(2,1)} %bitcast.257), channel_id=1, source_target_pairs={{0,2},{1,3},{2,0},{3,1},{4,6},{5,7},{6,4},{7,5},{8,10},{9,11},{10,... | collective-permute-start | bytes 884744 | tf_op jit(solution)/shard_map/ppermute | solution.py:770
  294.6 21.8 %collective-permute-start.27 = (f32[24,768]{1,0:T(8,128)S(1)}, f32[24,768]{1,0:T(8,128)S(1)}, u32[]{:S(2)}, u32[]{:S(2)}) collective-permute-start(f32[24,768]{1,0:T(8,128)S(1)} %broadcast_add_fusion), channel_id=1, source_target_pairs={{0,16},{1,17},{2,18},{3,19},{4,20},{5,21},{6,22},{7,23},{8,24},{9,... | collective-permute-start | bytes 221192 | tf_op jit(solution)/shard_map/ppermute | solution.py:785
  307.1 1.8 copy-start.17
  307.1 9.4 %collective-permute-start.28 = (f32[24,768]{1,0:T(8,128)S(1)}, f32[24,768]{1,0:T(8,128)S(1)}, u32[]{:S(2)}, u32[]{:S(2)}) collective-permute-start(f32[24,768]{1,0:T(8,128)S(1)} %broadcast_add_fusion), channel_id=1, source_target_pairs={{0,8},{1,9},{2,10},{3,11},{4,12},{5,13},{6,14},{7,15},{8,0},{9,1},... | collective-permute-start | bytes 221192 | tf_op jit(solution)/shard_map/ppermute | solution.py:785
  307.1 1.8 copy-start.16
  307.1 9.3 %collective-permute-start.29 = (f32[24,768]{1,0:T(8,128)S(1)}, f32[24,768]{1,0:T(8,128)S(1)}, u32[]{:S(2)}, u32[]{:S(2)}) collective-permute-start(f32[24,768]{1,0:T(8,128)S(1)} %broadcast_add_fusion), channel_id=1, source_target_pairs={{0,24},{1,25},{2,26},{3,27},{4,28},{5,29},{6,30},{7,31},{8,16},{9,... | collective-permute-start | bytes 221192 | tf_op jit(solution)/shard_map/ppermute | solution.py:785
  308.9 0.8 copy-start.14
  308.9 0.9 copy-start.15
  315.0 10.0 %collective-permute-start.21 = (bf16[1,1,2,2,1,24,1152]{6,5,3,2,4,1,0:T(8,128)(2,1)}, bf16[1,1,2,2,1,24,1152]{6,5,3,2,4,1,0:T(8,128)(2,1)S(1)}, u32[]{:S(2)}, u32[]{:S(2)}) collective-permute-start(bf16[1,1,2,2,1,24,1152]{6,5,3,2,4,1,0:T(8,128)(2,1)} %bitcast.259), channel_id=1, source_target_pairs={{0,1},{1,0},{2,3},{3,2},{4,5},{5,4},{6,7},{7,6},{8,9},{9,8},{10,11... | collective-permute-start | bytes 663560 | tf_op jit(solution)/shard_map/ppermute | solution.py:770
  315.8 11.6 %collective-permute-start.22 = (bf16[1,1,2,2,1,24,1152]{6,5,3,2,4,1,0:T(8,128)(2,1)}, bf16[1,1,2,2,1,24,1152]{6,5,3,2,4,1,0:T(8,128)(2,1)S(1)}, u32[]{:S(2)}, u32[]{:S(2)}) collective-permute-start(bf16[1,1,2,2,1,24,1152]{6,5,3,2,4,1,0:T(8,128)(2,1)} %bitcast.258), channel_id=1, source_target_pairs={{0,16},{1,17},{2,18},{3,19},{4,20},{5,21},{6,22},{7,23},{8,24},{9,... | collective-permute-start | bytes 663560 | tf_op jit(solution)/shard_map/ppermute | solution.py:770
  316.5 15.3 %collective-permute-start.30 = (f32[24,768]{1,0:T(8,128)S(1)}, f32[24,768]{1,0:T(8,128)S(1)}, u32[]{:S(2)}, u32[]{:S(2)}) collective-permute-start(f32[24,768]{1,0:T(8,128)S(1)} %add_add_fusion.2), channel_id=1, source_target_pairs={{0,1},{1,0},{2,3},{3,2},{4,5},{5,4},{6,7},{7,6},{8,9},{9,8},{10,11... | collective-permute-start | bytes 221192 | tf_op jit(solution)/shard_map/ppermute | solution.py:785
  317.6 14.2 %collective-permute-start.31 = (f32[24,768]{1,0:T(8,128)S(1)}, f32[24,768]{1,0:T(8,128)S(1)}, u32[]{:S(2)}, u32[]{:S(2)}) collective-permute-start(f32[24,768]{1,0:T(8,128)S(1)} %add_add_fusion.2), channel_id=1, source_target_pairs={{0,2},{1,3},{2,0},{3,1},{4,6},{5,7},{6,4},{7,5},{8,10},{9,11},{10,... | collective-permute-start | bytes 221192 | tf_op jit(solution)/shard_map/ppermute | solution.py:785
  319.3 12.6 %collective-permute-start.32 = (f32[24,768]{1,0:T(8,128)S(1)}, f32[24,768]{1,0:T(8,128)S(1)}, u32[]{:S(2)}, u32[]{:S(2)}) collective-permute-start(f32[24,768]{1,0:T(8,128)S(1)} %add_add_fusion.2), channel_id=1, source_target_pairs={{0,3},{1,2},{2,1},{3,0},{4,7},{5,6},{6,5},{7,4},{8,11},{9,10},{10,... | collective-permute-start | bytes 221192 | tf_op jit(solution)/shard_map/ppermute | solution.py:785
  325.1 2.9 copy-start.18
  325.1 17.3 %collective-permute-start.34 = (bf16[1,1,1,1,1,24,3840]{6,5,4,3,2,1,0:T(8,128)(2,1)}, bf16[1,1,1,1,1,24,3840]{6,5,4,3,2,1,0:T(8,128)(2,1)S(1)}, u32[]{:S(2)}, u32[]{:S(2)}) collective-permute-start(bf16[1,1,1,1,1,24,3840]{6,5,4,3,2,1,0:T(8,128)(2,1)} %bitcast.260), channel_id=1, source_target_pairs={{0,4},{1,5},{2,6},{3,7},{4,0},{5,1},{6,2},{7,3},{8,12},{9,13},{10,... | collective-permute-start | bytes 552968 | tf_op jit(solution)/shard_map/ppermute | solution.py:770
  327.5 14.8 %collective-permute-start.35 = (bf16[1,1,1,1,1,24,3072]{6,5,4,3,2,1,0:T(8,128)(2,1)}, bf16[1,1,1,1,1,24,3072]{6,5,4,3,2,1,0:T(8,128)(2,1)S(1)}, u32[]{:S(2)}, u32[]{:S(2)}) collective-permute-start(bf16[1,1,1,1,1,24,3072]{6,5,4,3,2,1,0:T(8,128)(2,1)} %bitcast.261), channel_id=1, source_target_pairs={{0,4},{1,5},{2,6},{3,7},{4,0},{5,1},{6,2},{7,3},{8,12},{9,13},{10,... | collective-permute-start | bytes 442376 | tf_op jit(solution)/shard_map/ppermute | solution.py:770
  331.1 14.4 %copy-start.30 = (bf16[2,24,1152]{2,1,0:T(8,128)(2,1)S(1)}, bf16[2,24,1152]{2,1,0:T(8,128)(2,1)}, u32[]{:S(2)}) copy-start(bf16[2,24,1152]{2,1,0:T(8,128)(2,1)} %get-tuple-element.174) | copy-start | bytes 331780
  331.1 14.9 %copy-start.29 = (bf16[2,24,1152]{2,1,0:T(8,128)(2,1)S(1)}, bf16[2,24,1152]{2,1,0:T(8,128)(2,1)}, u32[]{:S(2)}) copy-start(bf16[2,24,1152]{2,1,0:T(8,128)(2,1)} %get-tuple-element.176) | copy-start | bytes 331780
  331.9 15.7 %collective-permute-start.33 = (f32[24,768]{1,0:T(8,128)S(1)}, f32[24,768]{1,0:T(8,128)S(1)}, u32[]{:S(2)}, u32[]{:S(2)}) collective-permute-start(f32[24,768]{1,0:T(8,128)S(1)} %add_add_fusion.1), channel_id=1, source_target_pairs={{0,4},{1,5},{2,6},{3,7},{4,0},{5,1},{6,2},{7,3},{8,12},{9,13},{10,... | collective-permute-start | bytes 221192 | tf_op jit(solution)/shard_map/ppermute | solution.py:785
  342.3 0.7 copy-start.20
  345.5 4.7 %collective-permute-start.23 = (bf16[1,1,2,1,1,24,1152]{6,5,2,4,3,1,0:T(8,128)(2,1)S(1)}, bf16[1,1,2,1,1,24,1152]{6,5,2,4,3,1,0:T(8,128)(2,1)S(1)}, u32[]{:S(2)}, u32[]{:S(2)}) collective-permute-start(bf16[1,1,2,1,1,24,1152]{6,5,2,4,3,1,0:T(8,128)(2,1)S(1)} %bitcast.263), channel_id=1, source_target_pairs={{0,2},{1,3},{2,0},{3,1},{4,6},{5,7},{6,4},{7,5},{8,10},{9,11},{10,... | collective-permute-start | bytes 331784 | tf_op jit(solution)/shard_map/ppermute | solution.py:770
  346.0 5.5 %collective-permute-start.24 = (bf16[1,1,2,1,1,24,1152]{6,5,2,4,3,1,0:T(8,128)(2,1)S(1)}, bf16[1,1,2,1,1,24,1152]{6,5,2,4,3,1,0:T(8,128)(2,1)S(1)}, u32[]{:S(2)}, u32[]{:S(2)}) collective-permute-start(bf16[1,1,2,1,1,24,1152]{6,5,2,4,3,1,0:T(8,128)(2,1)S(1)} %bitcast.262), channel_id=1, source_target_pairs={{0,2},{1,3},{2,0},{3,1},{4,6},{5,7},{6,4},{7,5},{8,10},{9,11},{10,... | collective-permute-start | bytes 331784 | tf_op jit(solution)/shard_map/ppermute | solution.py:770
  350.3 1.2 copy-start.24
  354.7 6.7 %collective-permute-start.25 = (bf16[1,1,1,1,1,24,1152]{6,5,4,3,2,1,0:T(8,128)(2,1)}, bf16[1,1,1,1,1,24,1152]{6,5,4,3,2,1,0:T(8,128)(2,1)S(1)}, u32[]{:S(2)}, u32[]{:S(2)}) collective-permute-start(bf16[1,1,1,1,1,24,1152]{6,5,4,3,2,1,0:T(8,128)(2,1)} %bitcast.265), channel_id=1, source_target_pairs={{0,4},{1,5},{2,6},{3,7},{4,0},{5,1},{6,2},{7,3},{8,12},{9,13},{10,... | collective-permute-start | bytes 165896 | tf_op jit(solution)/shard_map/ppermute | solution.py:770
  358.6 5.3 %collective-permute-start.26 = (bf16[1,1,1,1,1,24,1152]{6,5,4,3,2,1,0:T(8,128)(2,1)}, bf16[1,1,1,1,1,24,1152]{6,5,4,3,2,1,0:T(8,128)(2,1)S(1)}, u32[]{:S(2)}, u32[]{:S(2)}) collective-permute-start(bf16[1,1,1,1,1,24,1152]{6,5,4,3,2,1,0:T(8,128)(2,1)} %bitcast.264), channel_id=1, source_target_pairs={{0,4},{1,5},{2,6},{3,7},{4,0},{5,1},{6,2},{7,3},{8,12},{9,13},{10,... | collective-permute-start | bytes 165896 | tf_op jit(solution)/shard_map/ppermute | solution.py:770
  (4 other events, 2.7 us)
Sparse Core Ops, SparseCore 0:
  11.0 93.1 all-gather.1
